TPU v7x, 128 devices: a whole 4x4x4 slice. The times are simulated.
128 devices in a mesh: seq: 8 (over x_lo, z), col: 16 (over y, x_hi, core).
Axes of the slice: x: 4 (x_hi: 2, x_lo: 2; x = x_hi * 2 + x_lo), y: 4, z: 4, core: 2. Of those that a mesh axis runs over, the one named last changes fastest.
Arguments:
- stream: bfloat16 [64, 1024, 768], P('seq', 'col'), may hold values from -40 to 40
- row_mask: int32 [64], replicated, may hold values from 0 to 1, as said below
- gain_row: bfloat16 [768], replicated, may hold values from 0.5 to 1.5
- row_query: bfloat16 [768, 768], replicated, may hold values from -13 to 13
- row_key: bfloat16 [768, 768], replicated, may hold values from -1 to 1
- row_value: bfloat16 [768, 768], replicated, may hold values from -0.875 to 0.875
- row_output: bfloat16 [768, 768], replicated, may hold values from -0.875 to 0.875
- gain_column: bfloat16 [768], replicated, may hold values from 0.5 to 1.5
- column_query: bfloat16 [768, 768], replicated, may hold values from -13 to 13
- column_key: bfloat16 [768, 768], replicated, may hold values from -1 to 1
- column_value: bfloat16 [768, 768], replicated, may hold values from -0.4375 to 0.4375
- column_output: bfloat16 [768, 768], replicated, may hold values from -0.4375 to 0.4375
- gain_feed: bfloat16 [768], replicated, may hold values from 0.5 to 1.5
- up_weight: bfloat16 [768, 3072], replicated, may hold values from -0.21875 to 0.21875
- down_weight: bfloat16 [3072, 768], replicated, may hold values from -0.109375 to 0.109375
Outputs:
- layer_out: bfloat16 [64, 1024, 768], P('seq', 'col')
Inputs may be any that keep to these rules, and one draw needn't show every extreme that they name: `row_mask`: sequence 0, the query sequence, is never padded.
All inputs are finite; a program needn't handle non-finite values.
Results may differ from a plain program's by a relative error of at most 0.015.
Values may be sent and summed in bfloat16 or wider, within the bound.
A program may use at most 128 MiB of HBM per device.

v0:
```python
import math

import jax
import jax.numpy as jnp
from jax import lax
from jax.sharding import PartitionSpec as P

H = 12


def layer_norm(values, gain):
    wide = values.astype(jnp.float32)
    center = wide - jnp.mean(wide, axis=-1, keepdims=True)
    spread = jnp.mean(center * center, axis=-1, keepdims=True)
    return center * lax.rsqrt(spread + 1e-05) * gain.astype(jnp.float32)


def column_attend(queries, key_rows, value_rows, row_mask, head_count):
    head_size = queries.shape[2] // head_count
    query_heads = queries.reshape(queries.shape[0], queries.shape[1], head_count, head_size)
    key_heads = key_rows.reshape(key_rows.shape[0], key_rows.shape[1], head_count, head_size)
    value_heads = value_rows.reshape(
        value_rows.shape[0], value_rows.shape[1], head_count, head_size
    )
    scores = jnp.einsum(
        "rchd,schd->chrs", query_heads, key_heads, preferred_element_type=jnp.float32
    ) * (1.0 / math.sqrt(head_size))
    live_keys = row_mask[None, None, None, :] > 0
    row_max = jnp.max(jnp.where(live_keys, scores, -1e30), axis=-1, keepdims=True)
    exponent = jnp.where(live_keys, jnp.exp(scores - row_max), 0.0)
    softmax_weights = (exponent / jnp.sum(exponent, axis=-1, keepdims=True)).astype(jnp.bfloat16)
    result = jnp.einsum(
        "chrs,schd->rchd", softmax_weights, value_heads, preferred_element_type=jnp.float32
    )
    return result.astype(jnp.bfloat16).reshape(queries.shape)


def local(
    stream,
    row_mask,
    gain_row,
    row_query,
    row_key,
    row_value,
    row_output,
    gain_column,
    column_query,
    column_key,
    column_value,
    column_output,
    gain_feed,
    up_weight,
    down_weight,
):
    rows_here, cols_here, model_width = stream.shape
    head_count = H
    head_size = model_width // head_count
    total_rows = row_mask.shape[0]
    offset = lax.axis_index("seq") * rows_here
    mask_here = lax.dynamic_slice_in_dim(row_mask, offset, rows_here, 0)
    flat_rows = stream.reshape(rows_here * cols_here, model_width)
    normed = layer_norm(flat_rows, gain_row).astype(jnp.bfloat16)

    def project(inputs, weight):
        return (
            jnp.dot(inputs, weight, preferred_element_type=jnp.float32)
            .astype(jnp.bfloat16)
            .reshape(rows_here, cols_here, model_width)
        )

    queries = project(normed, row_query) * mask_here.astype(jnp.bfloat16)[:, None, None]
    key_rows = project(normed, row_key)
    value_rows = project(normed, row_value)
    query_heads = queries.reshape(rows_here, cols_here, head_count, head_size)
    shard_piece = lax.all_gather(key_rows, "col", axis=1, tiled=True)
    piece_heads = shard_piece.reshape(
        shard_piece.shape[0], shard_piece.shape[1], head_count, head_size
    )
    partial_logits = jnp.einsum(
        "rihd,rjhd->hij", query_heads, piece_heads, preferred_element_type=jnp.float32
    )
    logit_scale = 1.0 / math.sqrt(head_size * total_rows)
    tied = lax.psum(partial_logits, "seq") * logit_scale
    weights = jax.nn.softmax(tied, axis=-1).astype(jnp.bfloat16)
    shard_piece = lax.all_gather(value_rows, "col", axis=1, tiled=True)
    piece_heads = shard_piece.reshape(
        shard_piece.shape[0], shard_piece.shape[1], head_count, head_size
    )
    row_mixed = jnp.einsum(
        "hij,rjhd->rihd", weights, piece_heads, preferred_element_type=jnp.float32
    )
    row_mixed = row_mixed.astype(jnp.bfloat16).reshape(rows_here * cols_here, model_width)
    after_row = (
        flat_rows.astype(jnp.float32)
        + jnp.dot(row_mixed, row_output, preferred_element_type=jnp.float32)
    ).astype(jnp.bfloat16)
    column_in = layer_norm(after_row, gain_column).astype(jnp.bfloat16)
    column_queries = project(column_in, column_query)
    column_keys = project(column_in, column_key)
    column_values = project(column_in, column_value)
    keys_whole, values_whole = (
        lax.all_gather(column_keys, "seq", axis=0, tiled=True),
        lax.all_gather(column_values, "seq", axis=0, tiled=True),
    )
    column_mixed = column_attend(column_queries, keys_whole, values_whole, row_mask, head_count)
    column_flat = column_mixed.reshape(rows_here * cols_here, model_width)
    after_column = (
        after_row.astype(jnp.float32)
        + jnp.dot(column_flat, column_output, preferred_element_type=jnp.float32)
    ).astype(jnp.bfloat16)
    feed_in = layer_norm(after_column, gain_feed).astype(jnp.bfloat16)
    hidden = jax.nn.gelu(
        jnp.dot(feed_in, up_weight, preferred_element_type=jnp.float32), approximate=False
    ).astype(jnp.bfloat16)
    layer_out = after_column.astype(jnp.float32) + jnp.dot(
        hidden, down_weight, preferred_element_type=jnp.float32
    )
    return layer_out.astype(jnp.bfloat16).reshape(rows_here, cols_here, model_width)


def solution(mesh):
    return jax.shard_map(
        local,
        mesh=mesh,
        in_specs=(
            P("seq", "col", None),
            P(),
            P(),
            P(),
            P(),
            P(),
            P(),
            P(),
            P(),
            P(),
            P(),
            P(),
            P(),
            P(),
            P(),
        ),
        out_specs=P("seq", "col", None),
        check_vma=False,
    )
```

profile of v0, /device:TPU:8, one launch (start us, length us, event | category | flops | bytes accessed | tf_op | source)
XLA Modules:
  0.0 523.5 jit_solution(7801385936003443411)
XLA Ops:
  6.5 1.5 convert_reduce_fusion.2
  8.0 1.5 fusion.53
  9.5 0.1 div.37
  9.6 0.7 convert_element_type.91
  10.3 0.1 rsqrt.28
  10.3 1.4 fusion.56
  11.8 0.8 convolution_convert_fusion.3
  12.6 1.3 copy.33
  13.9 0.0 all-gather.5.cloned.1.call-start
  14.0 2.0 convolution_convert_fusion.5
  16.0 1.4 copy.30
  17.4 0.0 all-reduce.2.cloned.1.call-start
  17.5 2.1 convolution_convert_fusion.4
  19.5 0.3 copy.32
  19.8 1.7 reshape.106
  21.5 0.1 dynamic-slice_convert_fusion
  21.6 1.6 broadcast_multiply_fusion
  23.2 82.4 %all-gather.7.cloned.1.call-done = bf16[8,1024,768]{2,0,1:T(8,128)(2,1)} async-done(((bf16[8,64,768]{2,0,1:T(8,128)(2,1)}), bf16[8,1024,768]{2,0,1:T(8,128)(2,1)}) %all-gather.7.cloned.1.call-update) | async-done | bytes 12582928 | tf_op jit(solution)/shard_map/all_gather | solution.py:75
  105.6 16.7 %copy.34 = bf16[8,1024,768]{1,2,0:T(8,128)(2,1)} copy(bf16[8,1024,768]{2,0,1:T(8,128)(2,1)} %all-gather.7.cloned.1.call-done) | data formatting | bytes 25165824 | tf_op jit(solution)/shard_map/all_gather | solution.py:75
  122.3 8.6 %fusion.29 = f32[12,64,1024]{2,1,0:T(8,128)} fusion(bf16[8,1024,12,64]{1,3,2,0:T(8,128)(2,1)} %bitcast.57, bf16[8,64,12,64]{1,0,3,2:T(8,128)(2,1)S(1)} %broadcast_multiply_fusion), kind=kOutput, calls=%fused_computation.45 | convolution fusion | flops 805306368 | bytes 16515072 | tf_op jit(solution)/shard_map/rihd,rjhd->hij/dot_general | solution.py:79
  130.9 0.3 all-gather.11.cloned.1.call-start
  131.3 0.3 copy-done.5
  131.6 65.0 %all-gather.5.cloned.1.call-done = bf16[8,1024,768]{2,0,1:T(8,128)(2,1)} async-done(((bf16[8,64,768]{2,0,1:T(8,128)(2,1)}), bf16[8,1024,768]{2,0,1:T(8,128)(2,1)}) %all-gather.5.cloned.1.call-update) | async-done | bytes 12582928 | tf_op jit(solution)/shard_map/all_gather | solution.py:85
  196.5 16.7 %copy.31 = bf16[8,1024,768]{1,2,0:T(8,128)(2,1)} copy(bf16[8,1024,768]{2,0,1:T(8,128)(2,1)} %all-gather.5.cloned.1.call-done) | data formatting | bytes 25165824 | tf_op jit(solution)/shard_map/all_gather | solution.py:85
  213.2 75.7 %all-reduce.2.cloned.1.call-done = f32[12,64,1024]{2,1,0:T(8,128)} async-done(((f32[12,64,1024]{2,1,0:T(8,128)}), f32[12,64,1024]{2,1,0:T(8,128)}) %all-reduce.2.cloned.1.call-update) | async-done | bytes 3145744 | tf_op jit(solution)/shard_map/psum | solution.py:83
  288.9 3.6 fusion.122
  292.6 8.1 %fusion.67 = bf16[8,64,12,64]{1,3,0,2:T(8,128)(2,1)S(1)} fusion(f32[12,64,1024]{2,1,0:T(8,128)S(1)} %get-tuple-element.6, f32[12,64]{1,0:T(8,128)S(1)} %get-tuple-element.5, bf16[8,1024,12,64]{1,3,2,0:T(8,128)(2,1)} %bitcast.58), kind=kOutput, calls=%fused_computation.79 | convolution fusion | flops 807272448 | bytes 16518144 | tf_op jit(solution)/shard_map/hij,rjhd->rihd/dot_general | solution.py:89
  300.7 1.2 copy.38
  301.9 1.7 reshape.109
  303.6 2.1 convert_reduce_fusion.1
  305.8 0.4 fusion.45
  306.2 1.7 convolution_convert_fusion
  307.9 0.6 all-gather.9.cloned.1.call-start
  308.5 3.0 convolution_convert_fusion.2
  311.5 2.1 convolution_convert_fusion.1
  313.7 1.3 reshape.118
  315.0 65.3 %all-gather.11.cloned.1.call-done = bf16[64,64,768]{2,1,0:T(8,128)(2,1)} async-done(((bf16[8,64,768]{2,1,0:T(8,128)(2,1)}), bf16[64,64,768]{2,1,0:T(8,128)(2,1)}) %all-gather.11.cloned.1.call-update) | async-done | bytes 6291472 | tf_op jit(solution)/shard_map/all_gather | solution.py:102
  380.2 19.6 %reshape.113 = bf16[64,64,12,64]{3,2,1,0:T(8,128)(2,1)} reshape(bf16[64,64,768]{2,1,0:T(8,128)(2,1)} %all-gather.11.cloned.1.call-done) | data formatting | bytes 12582912 | tf_op jit(solution)/shard_map/reshape | solution.py:21
  399.8 17.4 %fusion.4 = f32[64,12,8,64]{3,2,1,0:T(8,128)} fusion(bf16[64,64,12,64]{3,2,1,0:T(8,128)(2,1)} %reshape.113, bf16[8,64,12,64]{3,2,1,0:T(8,128)(2,1)S(1)} %reshape.118), kind=kOutput, calls=%fused_computation.4 | convolution fusion | flops 50331648 | bytes 8650752 | tf_op jit(solution)/shard_map/rchd,schd->chrs/dot_general | solution.py:25
  417.2 6.0 %fusion.123 = (f32[64,12,8]{2,1,0:T(8,128)S(1)}, f32[64,12,8,64]{3,2,1,0:T(8,128)}) fusion(f32[64,12,8,64]{3,2,1,0:T(8,128)} %fusion.4, pred[64]{0:T(512)(128)(4,1)S(1)} %broadcast_compare_fusion), kind=kOutput, calls=%fused_computation.133 | output fusion | flops 2359359 | bytes 3170368 | tf_op jit(solution)/shard_map/sub | solution.py:30
  423.2 29.6 %all-gather.9.cloned.1.call-done = bf16[64,64,768]{2,1,0:T(8,128)(2,1)} async-done(((bf16[8,64,768]{2,1,0:T(8,128)(2,1)}), bf16[64,64,768]{2,1,0:T(8,128)(2,1)}) %all-gather.9.cloned.1.call-update) | async-done | bytes 6291472 | tf_op jit(solution)/shard_map/all_gather | solution.py:103
  452.8 19.7 %reshape.111 = bf16[64,64,12,64]{3,2,1,0:T(8,128)(2,1)} reshape(bf16[64,64,768]{2,1,0:T(8,128)(2,1)} %all-gather.9.cloned.1.call-done) | data formatting | bytes 12582912 | tf_op jit(solution)/shard_map/reshape | solution.py:22
  472.6 15.6 %fusion.64 = bf16[8,64,12,64]{3,0,2,1:T(8,128)(2,1)} fusion(f32[64,12,8,64]{3,2,1,0:T(8,128)} %get-tuple-element.10, f32[64,12,8]{2,1,0:T(8,128)S(1)} %get-tuple-element.9, bf16[64,64,12,64]{3,2,1,0:T(8,128)(2,1)} %reshape.111), kind=kOutput, calls=%fused_computation.78 | convolution fusion | flops 51511296 | bytes 8675328 | tf_op jit(solution)/shard_map/chrs,schd->rchd/dot_general | solution.py:32
  488.2 3.0 copy.43
  491.2 1.2 reshape_reshape.7
  492.4 2.2 convert_reduce_fusion
  494.5 0.4 fusion.42
  494.9 21.8 %fusion.49 = bf16[512,768]{1,0:T(8,128)(2,1)} fusion(bf16[512,768]{1,0:T(8,128)(2,1)S(1)} %get-tuple-element.12, bf16[3072,768]{1,0:T(8,128)(2,1)} %param.29, bf16[768,3072]{1,0:T(8,128)(2,1)} %param.28, f32[768]{0:T(1024)S(1)} %convert_element_type.112, f32[512]{0:T(512)S(1)} %add_rsqrt_fusion.1, f32[512]{0:T(512)S(1)} %broadcast_multiply_fusion.2), kind=kOutput, calls=%fused_computation.59 | convolution fusion | flops 4937220096 | bytes 11017216 | tf_op jit(solution)/shard_map/dot_general | solution.py:115
  (34 shorter events, 0.2 us)
Async XLA Ops:
  6.5 297.1 %copy-start = (bf16[768,768]{1,0:T(8,128)(2,1)S(1)}, bf16[768,768]{1,0:T(8,128)(2,1)}, u32[]{:S(2)}) copy-start(bf16[768,768]{1,0:T(8,128)(2,1)} %param.21) | copy-start | bytes 3538948
  6.5 5.2 %copy-start.7 = (bf16[768,768]{1,0:T(8,128)(2,1)S(1)}, bf16[768,768]{1,0:T(8,128)(2,1)}, u32[]{:S(2)}) copy-start(bf16[768,768]{1,0:T(8,128)(2,1)} %param.19) | copy-start | bytes 3538948
  6.5 99.1 %all-gather.7.cloned.1.call-start = ((), (), s32[]{:S(2)}) async-start(), calls=%async_computation.1 | async-start | bytes 13369344 | tf_op jit(solution)/shard_map/all_gather | solution.py:75
  13.9 182.6 %all-gather.5.cloned.1.call-start = ((), (), s32[]{:S(2)}) async-start(), calls=%async_computation | async-start | bytes 13369344 | tf_op jit(solution)/shard_map/all_gather | solution.py:85
  17.4 271.5 %all-reduce.2.cloned.1.call-start = ((), (), s32[]{:S(2)}) async-start(), calls=%async_computation.2 | async-start | bytes 6291456 | tf_op jit(solution)/shard_map/psum | solution.py:83
  17.5 4.1 copy-start.9
  130.9 0.7 copy-start.5
  130.9 249.3 %all-gather.11.cloned.1.call-start = ((), (), s32[]{:S(2)}) async-start(), calls=%async_computation.4 | async-start | bytes 7077888 | tf_op jit(solution)/shard_map/all_gather | solution.py:102
  300.7 2.9 copy-start.2
  303.6 2.5 copy-start.8
  305.8 5.8 %copy-start.3 = (bf16[512,768]{1,0:T(8,128)(2,1)}, bf16[512,768]{1,0:T(8,128)(2,1)S(1)}, u32[]{:S(2)}) copy-start(bf16[512,768]{1,0:T(8,128)(2,1)S(1)} %get-tuple-element.8) | copy-start | bytes 2359300
  307.9 3.6 copy-start.6
  307.9 144.9 %all-gather.9.cloned.1.call-start = ((), (), s32[]{:S(2)}) async-start(), calls=%async_computation.3 | async-start | bytes 7077888 | tf_op jit(solution)/shard_map/all_gather | solution.py:103
  488.2 4.2 copy-start.4
  494.9 21.8 %copy-start.1 = (bf16[768,768]{1,0:T(8,128)(2,1)S(1)}, bf16[768,768]{1,0:T(8,128)(2,1)}, u32[]{:S(2)}) copy-start(bf16[768,768]{1,0:T(8,128)(2,1)} %param.21) | copy-start | bytes 3538948
Sparse Core Ops, SparseCore 0:
  14.0 91.5 all-gather.6
  108.1 88.4 all-gather.4
  199.1 89.8 all-reduce.1
  308.0 72.1 all-gather.10
  381.7 71.0 all-gather.8
where the time goes:
time: 532 us; the launch traced here: 524 us
  waiting for transfers between devices  318 us (60%)
  matrix products  87.5 us (16%)
  local copies, waits for them, and re-layouts  86.2 us (16%)
  other arithmetic  17.1 us (3%)
  between operations  13.6 us (3%)
    all_gather x1, waiting for transfers between devices, local(): shard_piece = lax.all_gather(key_rows, 'col', axis=1, tiled=True)  82.4 us
    psum x1, waiting for transfers between devices, local(): tied = lax.psum(partial_logits, 'seq') * logit_scale  75.7 us
    all_gather x1, waiting for transfers between devices, local(): lax.all_gather(column_keys, 'seq', axis=0, tiled=True)  65.3 us
    all_gather x1, waiting for transfers between devices, local(): shard_piece = lax.all_gather(value_rows, 'col', axis=1, tiled=True)  65 us
    all_gather x1, waiting for transfers between devices, local(): lax.all_gather(column_values, 'seq', axis=0, tiled=True)  29.6 us
    dot_general x1, matrix products, local(): jnp.dot(hidden, down_weight, preferred_element_type=jnp.float32)  21.8 us
    reshape x1, local copies, waits for them, and re-layouts, column_attend(): value_rows.reshape(value_rows.shape[0], value_rows.shape[1], head_count,...  19.7 us
    reshape x1, local copies, waits for them, and re-layouts, column_attend(): key_rows.reshape(key_rows.shape[0], key_rows.shape[1], head_count, head_s...  19.6 us
  transfers between devices with their start and end apart: 5, of which 5 were waited for; matrix products, arithmetic and copies ran while one was open for 19% of the time, Pallas kernels for 0%

commit v1 on v0

v1 whole, which is shorter than its diff:
```python
import math

import jax
import jax.numpy as jnp
from jax import lax
from jax.sharding import PartitionSpec as P

H = 12
DH = 64
Y_GROUPS = [[y * 4 + w for y in range(4)] for w in range(4)]
W_GROUPS = [[y * 4 + w for w in range(4)] for y in range(4)]


def layer_norm(values, gain):
    wide = values.astype(jnp.float32)
    center = wide - jnp.mean(wide, axis=-1, keepdims=True)
    spread = jnp.mean(center * center, axis=-1, keepdims=True)
    return center * lax.rsqrt(spread + 1e-05) * gain.astype(jnp.float32)


def dot(a, b):
    return jnp.dot(a, b, preferred_element_type=jnp.float32)


def local(
    stream,
    row_mask,
    gain_row,
    row_query,
    row_key,
    row_value,
    row_output,
    gain_column,
    column_query,
    column_key,
    column_value,
    column_output,
    gain_feed,
    up_weight,
    down_weight,
):
    rows, cols, width = stream.shape
    total = row_mask.shape[0]
    tokens = rows * cols
    hg = H // 4
    gw = hg * DH
    mask_here = lax.dynamic_slice_in_dim(row_mask, lax.axis_index("seq") * rows, rows, 0)
    flat = stream.reshape(tokens, width)
    normed = layer_norm(flat, gain_row).astype(jnp.bfloat16)

    def to_heads(weight, mask=None):
        out = dot(normed, weight).astype(jnp.bfloat16)
        if mask is not None:
            out = (out.reshape(rows, cols, width) * mask[:, None, None]).reshape(tokens, width)
        out = out.reshape(rows, cols, 4, gw).transpose(2, 0, 1, 3)
        return lax.all_to_all(out, "col", 0, 0, axis_index_groups=Y_GROUPS, tiled=True)

    q = to_heads(row_query, mask_here.astype(jnp.bfloat16))
    k = to_heads(row_key)
    v = to_heads(row_value)
    kk = lax.all_gather(k, "col", axis=0, axis_index_groups=W_GROUPS)
    vv = lax.all_gather(v, "col", axis=0, axis_index_groups=W_GROUPS)
    q5 = q.reshape(4, rows, cols, hg, DH)
    k5 = kk.reshape(4, 4, rows, cols, hg, DH)
    v5 = vv.reshape(4, 4, rows, cols, hg, DH)
    part = jnp.einsum("yrihd,wxrjhd->hyiwxj", q5, k5, preferred_element_type=jnp.float32)
    part = part.reshape(hg, 4 * cols, 16 * cols)
    tied = lax.psum_scatter(part, "seq", scatter_dimension=1, tiled=True)
    tied = tied * (1.0 / math.sqrt(DH * total))
    weights = jax.nn.softmax(tied, axis=-1).astype(jnp.bfloat16)
    weights = lax.all_gather(weights, "seq", axis=1, tiled=True)
    weights = weights.reshape(hg, 4, cols, 4, 4, cols)
    mixed = jnp.einsum("hyiwxj,wxrjhd->yrihd", weights, v5, preferred_element_type=jnp.float32)
    mixed = mixed.astype(jnp.bfloat16).reshape(4, rows, cols, gw)
    mixed = lax.all_to_all(mixed, "col", 0, 0, axis_index_groups=Y_GROUPS, tiled=True)
    mixed = mixed.transpose(1, 2, 0, 3).reshape(tokens, width)
    after_row = (flat.astype(jnp.float32) + dot(mixed, row_output)).astype(jnp.bfloat16)

    ns = total // rows
    cl = cols // ns
    moved = after_row.reshape(rows, ns, cl, width).transpose(1, 2, 0, 3)
    moved = lax.all_to_all(moved, "seq", 0, 0, tiled=True)
    x = moved.transpose(1, 0, 2, 3).reshape(tokens, width)
    column_in = layer_norm(x, gain_column).astype(jnp.bfloat16)
    cq = dot(column_in, column_query).astype(jnp.bfloat16).reshape(cl, total, H, DH)
    ck = dot(column_in, column_key).astype(jnp.bfloat16).reshape(cl, total, H, DH)
    cv = dot(column_in, column_value).astype(jnp.bfloat16).reshape(cl, total, H, DH)
    scores = jnp.einsum("crhd,cshd->chrs", cq, ck, preferred_element_type=jnp.float32) * (
        1.0 / math.sqrt(DH)
    )
    live = row_mask[None, None, None, :] > 0
    top = jnp.max(jnp.where(live, scores, -1e30), axis=-1, keepdims=True)
    ex = jnp.where(live, jnp.exp(scores - top), 0.0)
    cw = (ex / jnp.sum(ex, axis=-1, keepdims=True)).astype(jnp.bfloat16)
    cm = jnp.einsum("chrs,cshd->crhd", cw, cv, preferred_element_type=jnp.float32)
    cm = cm.astype(jnp.bfloat16).reshape(tokens, width)
    after_column = (x.astype(jnp.float32) + dot(cm, column_output)).astype(jnp.bfloat16)
    feed_in = layer_norm(after_column, gain_feed).astype(jnp.bfloat16)
    hidden = jax.nn.gelu(dot(feed_in, up_weight), approximate=False).astype(jnp.bfloat16)
    out = (after_column.astype(jnp.float32) + dot(hidden, down_weight)).astype(jnp.bfloat16)
    out = out.reshape(cl, ns, rows, width).transpose(1, 0, 2, 3)
    out = lax.all_to_all(out, "seq", 0, 0, tiled=True)
    return out.transpose(2, 0, 1, 3).reshape(rows, cols, width)


def solution(mesh):
    return jax.shard_map(
        local,
        mesh=mesh,
        in_specs=(P("seq", "col", None),) + (P(),) * 14,
        out_specs=P("seq", "col", None),
        check_vma=False,
    )
```

time: 532 us -> 362 us (0.68)
  waiting for transfers between devices: 318 us -> 121 us
  blocking collectives: 0 us -> 82.8 us
  matrix products: 87.5 us -> 55.4 us
  local copies, waits for them, and re-layouts: 86.2 us -> 69 us
  other arithmetic: 17.1 us -> 9.8 us
    all_gather x4 -> x3, waiting for transfers between devices: 242 us -> 88.6 us  [the longest x1 37.9 us: local(): vv = lax.all_gather(v, 'col', axis=0, axis_index_groups=W_GROUPS)]
    all_to_all x0 -> x5, blocking collectives: none -> 82.8 us  [the longest x3 55.2 us: to_heads(): lax.all_to_all(out, 'col', 0, 0, axis_index_groups=Y_GROUPS, tiled=True)]
    psum x1 -> x0, waiting for transfers between devices: 75.7 us -> none  [local(): tied = lax.psum(partial_logits, 'seq') * logit_scale]
    dot_general x13, matrix products: 87.5 us -> 55.4 us  [the longest x9 40.9 us: dot(): return jnp.dot(a, b, preferred_element_type=jnp.float32)]
    reduce_scatter x0 -> x1, waiting for transfers between devices: none -> 22.5 us  [local(): tied = lax.psum_scatter(part, 'seq', scatter_dimension=1, tiled=True)]
    all_gather x2, local copies, waits for them, and re-layouts: 33.3 us -> 15.8 us  [the longest x1 7.89 us: local(): kk = lax.all_gather(k, 'col', axis=0, axis_index_groups=W_GROUPS)]
    all_to_all x0 -> x1, waiting for transfers between devices: none -> 9.35 us  [local(): moved = lax.all_to_all(moved, 'seq', 0, 0, tiled=True)]
    reshape x6 -> x16, local copies, waits for them, and re-layouts: 45.4 us -> 36.4 us  [the longest x1 7.31 us: local(): part = part.reshape(hg, 4 * cols, 16 * cols)]
  transfers between devices with their start and end apart: 5 -> 5, of which waited for: 5 -> 5; matrix products, arithmetic and copies ran while one was open for 19% -> 5% of each run, Pallas kernels for 0% -> 0%
where the time goes in v1:
time: 362 us; the launch traced here: 355 us
  waiting for transfers between devices  121 us (33%)
  blocking collectives  82.8 us (23%)
  local copies, waits for them, and re-layouts  69 us (19%)
  matrix products  55.4 us (15%)
  between operations  13.6 us (4%)
  other arithmetic  9.8 us (3%)
  starting transfers between devices  4.06 us (1%)
    all_to_all x3, blocking collectives, to_heads(): lax.all_to_all(out, 'col', 0, 0, axis_index_groups=Y_GROUPS, tiled=True)  55.2 us
    dot_general x9, matrix products, dot(): return jnp.dot(a, b, preferred_element_type=jnp.float32)  40.9 us
    all_gather x1, waiting for transfers between devices, local(): vv = lax.all_gather(v, 'col', axis=0, axis_index_groups=W_GROUPS)  37.9 us
    all_gather x1, waiting for transfers between devices, local(): weights = lax.all_gather(weights, 'seq', axis=1, tiled=True)  33.8 us
    reduce_scatter x1, waiting for transfers between devices, local(): tied = lax.psum_scatter(part, 'seq', scatter_dimension=1, tiled=True)  22.5 us
    all_gather x1, waiting for transfers between devices, local(): kk = lax.all_gather(k, 'col', axis=0, axis_index_groups=W_GROUPS)  16.9 us
    all_to_all x1, blocking collectives, local(): lax.all_to_all(mixed, 'col', 0, 0, axis_index_groups=Y_GROUPS, tiled=True)  14.4 us
    all_to_all x1, blocking collectives, local(): out = lax.all_to_all(out, 'seq', 0, 0, tiled=True)  13.1 us
  transfers between devices with their start and end apart: 5, of which 5 were waited for; matrix products, arithmetic and copies ran while one was open for 5% of the time, Pallas kernels for 0%

profile of v1, /device:TPU:8, one launch (start us, length us, event | category | flops | bytes accessed | tf_op | source)
XLA Modules:
  0.0 355.3 jit_solution(12189017047559870427)
XLA Ops:
  6.5 1.4 convert_reduce_fusion.1
  8.0 1.5 fusion.43
  10.3 1.4 fusion.46
  12.6 2.0 convolution_convert_fusion.4
  14.7 0.9 reshape.148
  15.8 18.6 %all_to_all.30 = bf16[4,8,64,192]{3,2,1,0:T(8,128)(2,1)} all-to-all(bf16[4,8,64,192]{3,2,1,0:T(8,128)(2,1)S(1)} %bitcast.95), channel_id=1, replica_groups={{0,4,8,12},{1,5,9,13},{2,6,10,14},{3,7,11,15},{16,20,24,28},{17,21,25,2..., dimensions={0} | all-to-all | bytes 1572864 | tf_op jit(solution)/shard_map/all_to_all | solution.py:56
  34.4 2.0 convolution_convert_fusion.5
  36.5 0.9 reshape.146
  37.7 17.9 %all_to_all.31 = bf16[4,8,64,192]{3,2,1,0:T(8,128)(2,1)} all-to-all(bf16[4,8,64,192]{3,2,1,0:T(8,128)(2,1)S(1)} %fusion.61), channel_id=1, replica_groups={{0,4,8,12},{1,5,9,13},{2,6,10,14},{3,7,11,15},{16,20,24,28},{17,21,25,2..., dimensions={0} | all-to-all | bytes 1572864 | tf_op jit(solution)/shard_map/all_to_all | solution.py:56
  55.6 1.8 copy.46
  57.4 16.9 %all-gather.10.cloned.1.call-done = bf16[16,8,64,192]{3,2,1,0:T(8,128)(2,1)} async-done(((bf16[4,8,64,192]{3,2,1,0:T(8,128)(2,1)}), bf16[16,8,64,192]{3,2,1,0:T(8,128)(2,1)}) %all-gather.10.cloned.1.call-update) | async-done | bytes 3145744 | tf_op jit(solution)/shard_map/all_gather | solution.py:61
  74.3 7.9 %copy.48 = bf16[16,8,64,192]{2,3,1,0:T(8,128)(2,1)} copy(bf16[16,8,64,192]{3,2,1,0:T(8,128)(2,1)} %all-gather.10.cloned.1.call-done) | data formatting | bytes 6291456 | tf_op jit(solution)/shard_map/all_gather | solution.py:61
  82.2 4.6 %fusion.22 = f32[3,4,64,4,4,64]{5,2,4,3,1,0:T(8,128)S(1)} fusion(bf16[4,4,8,64,3,64,1]{3,5,4,2,1,0,6:T(8,128)(2,1)} %bitcast.91, bf16[4,8,64,3,64,1,1]{2,4,3,1,0,6,5:T(8,128)(2,1)S(1)} %bitcast.93), kind=kOutput, calls=%fused_computation.34 | convolution fusion | flops 805306368 | bytes 7077888 | tf_op jit(solution)/shard_map/yrihd,wxrjhd->hyiwxj/dot_general | solution.py:66
  86.8 6.7 %copy.51 = f32[3,4,64,4,4,64]{5,4,3,2,1,0:T(4,128)} copy(f32[3,4,64,4,4,64]{5,2,4,3,1,0:T(8,128)S(1)} %fusion.22) | data formatting | bytes 6291456 | tf_op jit(solution)/shard_map/yrihd,wxrjhd->hyiwxj/dot_general | solution.py:66
  93.6 7.3 %reshape.150 = f32[3,256,1024]{2,1,0:T(8,128)} reshape(f32[3,4,64,4,4,64]{5,4,3,2,1,0:T(4,128)} %copy.51) | data formatting | bytes 6291456 | tf_op jit(solution)/shard_map/reshape | solution.py:67
  100.9 1.1 copy-done.8
  102.0 2.0 convolution_convert_fusion.6
  104.1 0.9 reshape.144
  105.1 18.8 %all_to_all.32 = bf16[4,8,64,192]{3,2,1,0:T(8,128)(2,1)} all-to-all(bf16[4,8,64,192]{3,2,1,0:T(8,128)(2,1)S(1)} %bitcast.96), channel_id=1, replica_groups={{0,4,8,12},{1,5,9,13},{2,6,10,14},{3,7,11,15},{16,20,24,28},{17,21,25,2..., dimensions={0} | all-to-all | bytes 1572864 | tf_op jit(solution)/shard_map/all_to_all | solution.py:56
  124.2 22.5 %reduce-scatter.2.cloned.1.call-done = f32[3,32,1024]{2,1,0:T(8,128)} async-done(((f32[3,256,1024]{2,1,0:T(8,128)}), f32[3,32,1024]{2,1,0:T(8,128)}) %reduce-scatter.2.cloned.1.call-update) | async-done | bytes 393232 | tf_op jit(solution)/shard_map/reduce_scatter | solution.py:68
  146.7 1.9 fusion.60
  148.6 37.9 %all-gather.8.cloned.1.call-done = bf16[16,8,64,192]{3,2,1,0:T(8,128)(2,1)} async-done(((bf16[4,8,64,192]{3,2,1,0:T(8,128)(2,1)}), bf16[16,8,64,192]{3,2,1,0:T(8,128)(2,1)}) %all-gather.8.cloned.1.call-update) | async-done | bytes 3145744 | tf_op jit(solution)/shard_map/all_gather | solution.py:62
  186.5 7.9 %copy.44 = bf16[16,8,64,192]{2,3,1,0:T(8,128)(2,1)} copy(bf16[16,8,64,192]{3,2,1,0:T(8,128)(2,1)} %all-gather.8.cloned.1.call-done) | data formatting | bytes 6291456 | tf_op jit(solution)/shard_map/all_gather | solution.py:62
  194.4 33.8 %all-gather.6.cloned.1.call-done = bf16[3,256,1024]{2,1,0:T(8,128)(2,1)} async-done(((bf16[3,32,1024]{2,1,0:T(8,128)(2,1)}), bf16[3,256,1024]{2,1,0:T(8,128)(2,1)}) %all-gather.6.cloned.1.call-update) | async-done | bytes 1572880 | tf_op jit(solution)/shard_map/all_gather | solution.py:71
  228.2 6.6 %reshape.151 = bf16[3,4,64,4,4,64]{5,4,3,2,1,0:T(4,128)(2,1)} reshape(bf16[3,256,1024]{2,1,0:T(8,128)(2,1)} %all-gather.6.cloned.1.call-done) | data formatting | bytes 3145728 | tf_op jit(solution)/shard_map/reshape | solution.py:72
  234.8 6.5 %fusion.8 = bf16[3,8,64,4,64,1,1]{4,2,6,1,0,3,5:T(8,128)(2,1)S(1)} fusion(bf16[4,4,8,64,3,64,1]{3,5,4,2,1,0,6:T(8,128)(2,1)} %bitcast.92, bf16[3,4,64,4,4,64,1]{5,4,3,2,1,0,6:T(4,128)(2,1)} %bitcast.98), kind=kOutput, calls=%fused_computation.9 | convolution fusion | flops 805306368 | bytes 5505024 | tf_op jit(solution)/shard_map/hyiwxj,wxrjhd->yrihd/dot_general | solution.py:73
  241.5 1.6 copy.55
  243.1 14.4 %all_to_all.33 = bf16[4,8,64,192]{3,2,1,0:T(8,128)(2,1)S(1)} all-to-all(bf16[4,8,64,192]{3,2,1,0:T(8,128)(2,1)} %copy.55), channel_id=1, replica_groups={{0,4,8,12},{1,5,9,13},{2,6,10,14},{3,7,11,15},{16,20,24,28},{17,21,25,2..., dimensions={0} | all-to-all | bytes 1572864 | tf_op jit(solution)/shard_map/all_to_all | solution.py:75
  258.3 1.8 reshape.153
  260.2 2.3 fusion.47
  262.5 0.9 copy.135
  263.4 3.8 %all-to-all-start.4 = ((bf16[8,8,8,768]{3,1,2,0:T(8,128)(2,1)}), bf16[8,8,8,768]{3,1,2,0:T(8,128)(2,1)S(1)}, u32[]{:S(2)}, u32[]{:S(2)}) async-start(bf16[8,8,8,768]{3,1,2,0:T(8,128)(2,1)} %bitcast.90), calls=%async_computation.5 | async-start | bytes 1572864 | tf_op jit(solution)/shard_map/all_to_all | solution.py:82
  267.3 9.3 %all-to-all-done.4 = bf16[8,8,8,768]{3,1,2,0:T(8,128)(2,1)S(1)} async-done(((bf16[8,8,8,768]{3,1,2,0:T(8,128)(2,1)}), bf16[8,8,8,768]{3,1,2,0:T(8,128)(2,1)S(1)}, u32[]{:S(2)}, u32[]{:S(2)}) %all-to-all-start.4) | async-done | bytes 786464 | tf_op jit(solution)/shard_map/all_to_all | solution.py:82
  279.3 0.9 copy-done.9
  280.2 2.9 convolution_convert_fusion.2
  283.1 2.7 reshape.174
  285.8 3.2 convolution_convert_fusion.1
  289.0 3.8 %reshape.175 = bf16[8,64,12,64]{3,2,1,0:T(8,128)(2,1)} reshape(bf16[512,768]{1,0:T(8,128)(2,1)} %convolution_convert_fusion.1) | data formatting | bytes 1572864 | tf_op jit(solution)/shard_map/reshape | solution.py:86
  292.8 3.2 convolution_convert_fusion.3
  296.0 3.8 %reshape.173 = bf16[8,64,12,64]{3,2,1,0:T(8,128)(2,1)} reshape(bf16[512,768]{1,0:T(8,128)(2,1)} %convolution_convert_fusion.3) | data formatting | bytes 1572864 | tf_op jit(solution)/shard_map/reshape | solution.py:87
  299.8 2.5 fusion.33
  302.3 1.3 fusion.117
  304.7 2.4 copy.71
  307.2 3.7 %reshape.158 = bf16[512,768]{0,1:T(8,128)(2,1)} reshape(bf16[8,64,12,64]{1,0,3,2:T(8,128)(2,1)} %copy.71) | data formatting | bytes 1572864 | tf_op jit(solution)/shard_map/reshape | solution.py:96
  310.9 2.0 convert_reduce_fusion
  313.3 21.1 %fusion.32 = bf16[512,768]{1,0:T(8,128)(2,1)S(1)} fusion(bf16[512,768]{1,0:T(8,128)(2,1)S(1)} %get-tuple-element.8, bf16[3072,768]{1,0:T(8,128)(2,1)} %param.29, bf16[768,3072]{1,0:T(8,128)(2,1)} %param.28, f32[768]{0:T(1024)S(1)} %convert_element_type.126, f32[512]{0:T(512)S(1)} %add_rsqrt_fusion.1, f32[512]{0:T(512)S(1)} %broadcast_multiply_fusion.1), kind=kOutput, calls=%fused_computation.44 | convolution fusion | flops 4937220096 | bytes 11017216 | tf_op jit(solution)/shard_map/dot_general | solution.py:22
  334.5 13.1 %all_to_all.34 = bf16[8,8,8,768]{3,2,1,0:T(8,128)(2,1)S(1)} all-to-all(bf16[8,8,8,768]{3,2,1,0:T(8,128)(2,1)S(1)} %bitcast.99), channel_id=1, replica_groups=mesh['seq'=8,'col'=16] {'seq'}, dimensions={0} | all-to-all | bytes 1572864 | tf_op jit(solution)/shard_map/all_to_all | solution.py:102
  347.6 1.0 copy.73
  (63 shorter events, 7.9 us)
Async XLA Ops:
  6.5 304.3 %copy-start = (bf16[768,768]{1,0:T(8,128)(2,1)S(1)}, bf16[768,768]{1,0:T(8,128)(2,1)}, u32[]{:S(2)}) copy-start(bf16[768,768]{1,0:T(8,128)(2,1)} %param.26) | copy-start | bytes 3538948
  6.5 67.8 %all-gather.10.cloned.1.call-start = ((), (), s32[]{:S(2)}) async-start(), calls=%async_computation.10 | async-start | bytes 5242880 | tf_op jit(solution)/shard_map/all_gather | solution.py:61
  11.7 0.9 copy-start.6
  15.8 18.7 %copy-start.7 = (bf16[512,768]{1,0:T(8,128)(2,1)S(1)}, bf16[512,768]{1,0:T(8,128)(2,1)}, u32[]{:S(2)}) copy-start(bf16[512,768]{1,0:T(8,128)(2,1)} %copy-done.6) | copy-start | bytes 2359300
  34.3 3.1 copy-start.12
  34.4 112.3 %reduce-scatter.2.cloned.1.call-start = ((), (), s32[]{:S(2)}) async-start(), calls=%async_computation.7 | async-start | bytes 3538944 | tf_op jit(solution)/shard_map/reduce_scatter | solution.py:68
  100.9 1.1 copy-start.8
  100.9 85.6 %all-gather.8.cloned.1.call-start = ((), (), s32[]{:S(2)}) async-start(), calls=%async_computation.9 | async-start | bytes 5242880 | tf_op jit(solution)/shard_map/all_gather | solution.py:62
  123.9 104.3 %all-gather.6.cloned.1.call-start = ((), (), s32[]{:S(2)}) async-start(), calls=%async_computation.8 | async-start | bytes 1769472 | tf_op jit(solution)/shard_map/all_gather | solution.py:71
  243.1 17.0 %copy-start.2 = (bf16[8,64,768]{2,1,0:T(8,128)(2,1)S(1)}, bf16[8,64,768]{2,1,0:T(8,128)(2,1)}, u32[]{:S(2)}) copy-start(bf16[8,64,768]{2,1,0:T(8,128)(2,1)} %param.15) | copy-start | bytes 2359300
  260.2 7.0 %copy-start.10 = (bf16[768]{0:T(1024)(128)(2,1)S(1)}, bf16[768]{0:T(1024)(128)(2,1)}, u32[]{:S(2)}) copy-start(bf16[768]{0:T(1024)(128)(2,1)} %param.22) | copy-start | bytes 4612
  260.2 7.0 %copy-start.11 = (bf16[768]{0:T(1024)(128)(2,1)S(1)}, bf16[768]{0:T(1024)(128)(2,1)}, u32[]{:S(2)}) copy-start(bf16[768]{0:T(1024)(128)(2,1)} %param.27) | copy-start | bytes 4612
  263.4 13.2 %all-to-all-start.4 = ((bf16[8,8,8,768]{3,1,2,0:T(8,128)(2,1)}), bf16[8,8,8,768]{3,1,2,0:T(8,128)(2,1)S(1)}, u32[]{:S(2)}, u32[]{:S(2)}) async-start(bf16[8,8,8,768]{3,1,2,0:T(8,128)(2,1)} %bitcast.90), calls=%async_computation.5 | async-start | bytes 1572864 | tf_op jit(solution)/shard_map/all_to_all | solution.py:82
  278.1 1.2 copy-start.3
  279.3 0.9 copy-start.9
  302.3 1.6 copy-start.5
  304.7 6.1 %copy-start.4 = (f32[8,8,8,768]{3,2,1,0:T(8,128)S(1)}, f32[8,8,8,768]{3,2,1,0:T(8,128)}, u32[]{:S(2)}) copy-start(f32[8,8,8,768]{3,2,1,0:T(8,128)} %copy-done.3) | copy-start | bytes 4718596
  313.3 35.4 %copy-start.1 = (bf16[768,768]{1,0:T(8,128)(2,1)S(1)}, bf16[768,768]{1,0:T(8,128)(2,1)}, u32[]{:S(2)}) copy-start(bf16[768,768]{1,0:T(8,128)(2,1)} %param.26) | copy-start | bytes 3538948
Sparse Core Ops, SparseCore 0:
  34.5 39.7 all-gather.9
  101.0 45.6 reduce-scatter.1
  148.4 38.0 all-gather.7
  188.0 40.1 all-gather.5

commit v2 on v1

v2 whole, which is shorter than its diff:
```python
import functools

import jax
import jax.numpy as jnp
from jax import lax
from jax.experimental import pallas as pl
from jax.experimental.pallas import tpu as pltpu
from jax.sharding import PartitionSpec as P

D = 768
H = 12
DH = 64
FF = 3072
RL = 8
CL = 64
T = RL * CL
NS = 8
NY = 4
NW = 4
HG = H // NY
BF = jnp.bfloat16
F32 = jnp.float32
MESH = pl.DeviceIdType.MESH
VMEM_LIMIT = 56 * 1024 * 1024


def norm(wide, gain):
    center = wide - jnp.mean(wide, axis=-1, keepdims=True)
    spread = jnp.mean(center * center, axis=-1, keepdims=True)
    return center * lax.rsqrt(spread + 1e-05) * gain


def dot(a, b, dims=((1,), (0,))):
    return lax.dot_general(a, b, (dims, ((), ())), preferred_element_type=F32)


def place():
    s = lax.axis_index("seq")
    col = lax.axis_index("col")
    return s, lax.div(col, NW), lax.rem(col, NW)


def remote(src, dst, send, recv, s, col):
    return pltpu.make_async_remote_copy(
        src_ref=src, dst_ref=dst, send_sem=send, recv_sem=recv, device_id=(s, col), device_id_type=MESH
    )


def greet(peers):
    barrier = pltpu.get_barrier_semaphore()
    for s, col in peers:
        pl.semaphore_signal(barrier, inc=1, device_id=(s, col), device_id_type=MESH)
    pl.semaphore_wait(barrier, len(peers))


def pair_lanes(a, b):
    low = lax.broadcasted_iota(jnp.int32, a.shape, 1) < DH
    return jnp.where(low, a, pltpu.roll(b, DH, 1)), jnp.where(low, pltpu.roll(a, DH, 1), b)


def row_kernel(
    mask, x, gain, wq_h, wk_h, wv_h, wo_h, out,
    wk, wq, wv, wo, xn, acc, pk, qb, kb, vb, part, rs, pw, mxs, mxr, cs,
    wsem, ysend, yrecv, wsend, wrecv, rsend, rrecv, psend, precv, msend, mrecv, csend, crecv,
):
    s, y, w = place()
    col = y * NW + w
    ycol = [None] + [lax.rem(y + d, NY) * NW + w for d in range(1, NY)]
    yidx = [None] + [lax.rem(y + d, NY) for d in range(1, NY)]
    sidx = [None] + [lax.rem(s + d, NS) for d in range(1, NS)]
    w_far = lax.rem(w + 2, NW)
    w_core = w + 1 - 2 * lax.rem(w, 2)
    w_diag = lax.rem(w_core + 2, NW)
    far, core = y * NW + w_far, y * NW + w_core

    loads = []
    for i, (h, v) in enumerate(((wk_h, wk), (wq_h, wq), (wv_h, wv), (wo_h, wo))):
        loads.append(pltpu.make_async_copy(h, v, wsem.at[i]))
        loads[-1].start()
    greet([(s, c) for c in ycol[1:]] + [(s, far), (s, core)] + [(d, col) for d in sidx[1:]])

    xn[...] = norm(x[...].astype(F32), gain[...].astype(F32)).astype(BF)
    sends = []

    def project(kind, weight, load, into, base, masked=False):
        load.wait()
        acc[...] = dot(xn[...], weight[...])
        for p in range(RL // 2):
            for hp in range(H // 2):
                a = acc[2 * p * CL:(2 * p + 1) * CL, hp * 128:(hp + 1) * 128]
                b = acc[(2 * p + 1) * CL:(2 * p + 2) * CL, hp * 128:(hp + 1) * 128]
                if masked:
                    a = a * mask[s * RL + 2 * p].astype(F32)
                    b = b * mask[s * RL + 2 * p + 1].astype(F32)
                first, second = pair_lanes(a, b)
                pk[kind, 2 * hp, :, p * 128:(p + 1) * 128] = first.astype(BF)
                pk[kind, 2 * hp + 1, :, p * 128:(p + 1) * 128] = second.astype(BF)
        rows = pl.ds(pl.multiple_of(base, CL), CL)
        copies = []
        for g in range(HG):
            group = []
            for d in range(1, NY):
                c = remote(
                    pk.at[kind, yidx[d] * HG + g], into.at[g, rows],
                    ysend.at[kind, g, d - 1], yrecv.at[kind, g, d - 1], s, ycol[d],
                )
                c.start()
                group.append(c)
                sends.append(c)
            into[g, rows, :] = pk[kind, y * HG + g]
            copies.append(group)
        return copies

    def block(ref, g, index):
        return ref.at[g, pl.ds(pl.multiple_of(index * 256, 256), 256)]

    def spread(kind, ref, copies):
        out_copies = []
        for g in range(HG):
            for c in copies[g]:
                c.wait_recv()
            a = remote(block(ref, g, w), block(ref, g, w), wsend.at[kind, g, 0], wrecv.at[kind, g, 0], s, far)
            b = remote(block(ref, g, w), block(ref, g, w), wsend.at[kind, g, 1], wrecv.at[kind, g, 1], s, core)
            a.start()
            b.start()
            sends.extend((a, b))
            out_copies.append((a, b))
        return out_copies

    def relay(kind, ref, copies, g):
        a, b = copies[g]
        a.wait_recv()
        c = remote(block(ref, g, w_far), block(ref, g, w_far), wsend.at[kind, g, 2], wrecv.at[kind, g, 2], s, core)
        c.start()
        sends.append(c)
        b.wait_recv()
        return c

    ky = project(0, wk, loads[0], kb, (w * NY + y) * CL)
    qy = project(1, wq, loads[1], qb, y * CL, masked=True)
    kw = spread(0, kb, ky)
    vy = project(2, wv, loads[2], vb, (w * NY + y) * CL)

    rcopies = []
    for g in range(HG):
        c = relay(0, kb, kw, g)
        for q in qy[g]:
            q.wait_recv()
        c.wait_recv()
        for j in range(4):
            part[g, :, j * 256:(j + 1) * 256] = dot(qb[g], kb[g, j * 256:(j + 1) * 256, :], ((1,), (1,)))
        group = []
        for d in range(1, NS):
            c = remote(
                part.at[g, pl.ds(pl.multiple_of(sidx[d] * 32, 32), 32)], rs.at[g, d - 1],
                rsend.at[g, d - 1], rrecv.at[g, d - 1], sidx[d], col,
            )
            c.start()
            group.append(c)
            sends.append(c)
        rcopies.append(group)

    vw = spread(1, vb, vy)
    pcopies = []
    mine = pl.ds(pl.multiple_of(s * 32, 32), 32)
    for g in range(HG):
        for c in rcopies[g]:
            c.wait_recv()
        total = part[g, mine, :]
        for d in range(NS - 1):
            total = total + rs[g, d]
        total = total * (1.0 / 64.0)
        e = jnp.exp(total - jnp.max(total, axis=-1, keepdims=True))
        pw[g, mine, :] = (e / jnp.sum(e, axis=-1, keepdims=True)).astype(BF)
        group = []
        for d in range(1, NS):
            c = remote(pw.at[g, mine], pw.at[g, mine], psend.at[g, d - 1], precv.at[g, d - 1], sidx[d], col)
            c.start()
            group.append(c)
            sends.append(c)
        pcopies.append(group)
    vd = [relay(1, vb, vw, g) for g in range(HG)]

    mcopies = []
    for g in range(HG):
        vd[g].wait_recv()
        for c in pcopies[g]:
            c.wait_recv()
        mxs[g] = dot(pw[g], vb[g]).astype(BF)
        for d in range(1, NY):
            c = remote(
                mxs.at[g, pl.ds(pl.multiple_of(yidx[d] * CL, CL), CL)], mxr.at[y * HG + g],
                msend.at[g, d - 1], mrecv.at[g, d - 1], s, ycol[d],
            )
            c.start()
            mcopies.append(c)
            sends.append(c)
        mxr[y * HG + g] = mxs[g, pl.ds(pl.multiple_of(y * CL, CL), CL), :]
    for c in mcopies:
        c.wait_recv()
    for p in range(RL // 2):
        for hp in range(H // 2):
            a = mxr[2 * hp, :, p * 128:(p + 1) * 128].astype(F32)
            b = mxr[2 * hp + 1, :, p * 128:(p + 1) * 128].astype(F32)
            first, second = pair_lanes(a, b)
            xn[2 * p * CL:(2 * p + 1) * CL, hp * 128:(hp + 1) * 128] = first.astype(BF)
            xn[(2 * p + 1) * CL:(2 * p + 2) * CL, hp * 128:(hp + 1) * 128] = second.astype(BF)
    loads[3].wait()
    acc[...] = x[...].astype(F32) + dot(xn[...], wo[...])
    ccopies = []
    for t in range(NS):
        rows = [acc[r * CL + t * RL:r * CL + (t + 1) * RL, :] for r in range(RL)]
        cs[t] = jnp.concatenate(rows, axis=0).astype(BF)
    for d in range(1, NS):
        c = remote(cs.at[sidx[d]], out.at[s], csend.at[d - 1], crecv.at[d - 1], sidx[d], col)
        c.start()
        ccopies.append(c)
        sends.append(c)
    out[s] = cs[s]
    for c in ccopies:
        c.wait_recv()
    for c in sends:
        c.wait_send()


def col_kernel(
    mask, x, gc, gf, wq_h, wk_h, wv_h, wo_h, up_h, dn_h, out,
    wq, wk, wv, wo, up, dn, xf, xo, cin, qc, kc, vc, hb, facc, cs, cr,
    wsem, csend, crecv,
):
    s, y, w = place()
    col = y * NW + w
    sidx = [None] + [lax.rem(s + d, NS) for d in range(1, NS)]
    loads = []
    for i, (h, v) in enumerate(((wq_h, wq), (wk_h, wk), (wv_h, wv), (wo_h, wo), (up_h, up), (dn_h, dn))):
        loads.append(pltpu.make_async_copy(h, v, wsem.at[i]))
        loads[-1].start()
    greet([(d, col) for d in sidx[1:]])

    for j in range(D // 128):
        xf[j] = x[:, j * 128:(j + 1) * 128].astype(F32)
    for c in range(RL):
        xc = jnp.concatenate([xf[j, pl.ds(c, 64, stride=RL), :] for j in range(D // 128)], axis=1)
        xo[c * 64:(c + 1) * 64, :] = xc
        cin[c * 64:(c + 1) * 64, :] = norm(xc, gc[...].astype(F32)).astype(BF)
    for load, weight, into in ((loads[0], wq, qc), (loads[1], wk, kc), (loads[2], wv, vc)):
        load.wait()
        into[...] = dot(cin[...], weight[...]).astype(BF)

    live = mask[...] > 0
    lane = lax.broadcasted_iota(jnp.int32, (1, 256), 1)
    pick = [((lane >= h * 64) & (lane < (h + 1) * 64)).astype(F32) for h in range(4)]

    @pl.loop(0, RL)
    def _(c):
        rows = pl.ds(pl.multiple_of(c * 64, 64), 64)
        for g in range(3):
            lanes = slice(g * 256, (g + 1) * 256)
            q = qc[rows, lanes]
            qe = jnp.concatenate([q * pick[h].astype(BF) for h in range(4)], axis=0)
            st = dot(kc[rows, lanes], qe, ((1,), (1,))) * 0.125
            st = jnp.where(live, st, -1e30)
            e = jnp.exp(st - jnp.max(st, axis=0, keepdims=True))
            p = (e / jnp.sum(e, axis=0, keepdims=True)).astype(BF)
            res = dot(p, vc[rows, lanes], ((0,), (0,)))
            mixed = res[0:64] * pick[0]
            for h in range(1, 4):
                mixed = mixed + res[h * 64:(h + 1) * 64] * pick[h]
            cin[rows, lanes] = mixed.astype(BF)

    loads[3].wait()
    after = (xo[...] + dot(cin[...], wo[...])).astype(BF).astype(F32)
    facc[...] = after
    cin[...] = norm(after, gf[...].astype(F32)).astype(BF)
    loads[4].wait()
    loads[5].wait()

    @pl.loop(0, FF // D)
    def _(n):
        part = pl.ds(pl.multiple_of(n * D, D), D)
        h = dot(cin[...], up[:, part])
        hb[...] = (0.5 * h * (1.0 + lax.erf(h * 0.7071067811865476))).astype(BF)
        facc[...] += dot(hb[...], dn[part, :])

    for j in range(D // 128):
        lanes = slice(j * 128, (j + 1) * 128)
        for c in range(RL):
            xf[j, pl.ds(c, 64, stride=RL), :] = facc[c * 64:(c + 1) * 64, lanes]
        for t in range(NS):
            cs[t, :, lanes] = xf[j, t * 64:(t + 1) * 64, :].astype(BF)
    copies = []
    for d in range(1, NS):
        c = remote(cs.at[sidx[d]], cr.at[s], csend.at[d - 1], crecv.at[d - 1], sidx[d], col)
        c.start()
        copies.append(c)
    cr[s] = cs[s]
    for c in copies:
        c.wait_recv()
    for m in range(NS // 2):
        a = cr[2 * m].astype(F32)
        b = cr[2 * m + 1].astype(F32)
        for r in range(RL):
            both = jnp.concatenate([a[r * 8:(r + 1) * 8], b[r * 8:(r + 1) * 8]], axis=0)
            out[r * CL + m * 16:r * CL + (m + 1) * 16, :] = both.astype(BF)
    for c in copies:
        c.wait_send()


def vmem():
    return pl.BlockSpec(memory_space=pltpu.VMEM)


def hbm():
    return pl.BlockSpec(memory_space=pl.ANY)


def dma(*shape):
    return pltpu.SemaphoreType.DMA(shape)


def local(
    stream, row_mask, gain_row, row_query, row_key, row_value, row_output,
    gain_column, column_query, column_key, column_value, column_output,
    gain_feed, up_weight, down_weight,
):
    x = stream.reshape(T, D)
    weight = pltpu.VMEM((D, D), BF)
    moved = pl.pallas_call(
        row_kernel,
        out_shape=jax.ShapeDtypeStruct((NS, 64, D), BF),
        in_specs=[pl.BlockSpec(memory_space=pltpu.SMEM), vmem(), vmem()] + [hbm()] * 4,
        out_specs=vmem(),
        scratch_shapes=[
            weight, weight, weight, weight,
            pltpu.VMEM((T, D), BF),
            pltpu.VMEM((T, D), F32),
            pltpu.VMEM((3, H, CL, 512), BF),
            pltpu.VMEM((HG, 256, 512), BF),
            pltpu.VMEM((HG, 1024, 512), BF),
            pltpu.VMEM((HG, 1024, 512), BF),
            pltpu.VMEM((HG, 256, 1024), F32),
            pltpu.VMEM((HG, NS - 1, 32, 1024), F32),
            pltpu.VMEM((HG, 256, 1024), BF),
            pltpu.VMEM((HG, 256, 512), BF),
            pltpu.VMEM((H, CL, 512), BF),
            pltpu.VMEM((NS, 64, D), BF),
            dma(4),
            dma(3, HG, NY - 1), dma(3, HG, NY - 1),
            dma(2, HG, 3), dma(2, HG, 3),
            dma(HG, NS - 1), dma(HG, NS - 1),
            dma(HG, NS - 1), dma(HG, NS - 1),
            dma(HG, NY - 1), dma(HG, NY - 1),
            dma(NS - 1), dma(NS - 1),
        ],
        compiler_params=pltpu.CompilerParams(
            collective_id=0, has_side_effects=True, vmem_limit_bytes=VMEM_LIMIT
        ),
        name="row_attention",
    )(row_mask, x, gain_row.reshape(1, D), row_query, row_key, row_value, row_output)
    out = pl.pallas_call(
        col_kernel,
        out_shape=jax.ShapeDtypeStruct((T, D), BF),
        in_specs=[vmem()] * 4 + [hbm()] * 6,
        out_specs=vmem(),
        scratch_shapes=[
            weight, weight, weight, weight,
            pltpu.VMEM((D, FF), BF),
            pltpu.VMEM((FF, D), BF),
            pltpu.VMEM((D // 128, T, 128), F32),
            pltpu.VMEM((T, D), F32),
            pltpu.VMEM((T, D), BF),
            pltpu.VMEM((T, D), BF),
            pltpu.VMEM((T, D), BF),
            pltpu.VMEM((T, D), BF),
            pltpu.VMEM((T, D), BF),
            pltpu.VMEM((T, D), F32),
            pltpu.VMEM((NS, 64, D), BF),
            pltpu.VMEM((NS, 64, D), BF),
            dma(6),
            dma(NS - 1), dma(NS - 1),
        ],
        compiler_params=pltpu.CompilerParams(
            collective_id=1, has_side_effects=True, vmem_limit_bytes=VMEM_LIMIT
        ),
        name="column_and_feed",
    )(
        row_mask.reshape(64, 1), moved.reshape(T, D), gain_column.reshape(1, D), gain_feed.reshape(1, D),
        column_query, column_key, column_value, column_output, up_weight, down_weight,
    )
    return out.reshape(RL, CL, D)


def solution(mesh):
    return jax.shard_map(
        local,
        mesh=mesh,
        in_specs=(P("seq", "col", None),) + (P(),) * 14,
        out_specs=P("seq", "col", None),
        check_vma=False,
    )
```

time: 362 us -> 161 us (0.44)
  the two profiles are of different devices: /device:TPU:8 before, /device:TPU:1 now
where the time goes in v2:
time: 161 us
  Pallas kernels  154 us (96%)
  local copies, waits for them, and re-layouts  7.22 us (4%)
    pallas_call x1, Pallas kernels, local(): pl.pallas_call(row_kernel, out_shape=jax.ShapeDtypeStruct((NS, 64, D), BF...  118 us
    pallas_call x1, Pallas kernels, local(): pl.pallas_call(col_kernel, out_shape=jax.ShapeDtypeStruct((T, D), BF), in...  35.6 us

profile of v2, /device:TPU:1, one launch (start us, length us, event | category | flops | bytes accessed | tf_op | source)
XLA Modules:
  0.0 161.0 jit_solution(9479003692382013335)
XLA Ops:
  0.0 1.3 reshape.23.gain
  1.3 1.3 reshape.25.gc
  2.5 1.3 reshape.26.gf
  3.8 1.4 copy.16.mask
  5.2 118.1 %row_attention.1 = bf16[8,64,768]{2,1,0:T(8,128)(2,1)} custom-call(s32[64]{0:T(128)} %mask.1, bf16[512,768]{1,0:T(8,128)(2,1)} %bitcast.6, bf16[1,768]{1,0:T(2,128)(2,1)} %reshape.23.gain, bf16[768,768]{1,0:T(8,128)(2,1)} %wq_h.2, bf16[768,768]{1,0:T(8,128)(2,1)} %wk_h.2, bf16[768,768]{1,0:T(8,128)(2,1)} %wv_h.2, bf16[768,768]{1,0:T(8,128)(2,1)} %wo_h.2), custom_call_target="tpu_custom_call" | custom-call | tf_op jit(solution)/shard_map/row_attention/pallas_call | solution.py:328
  123.3 35.6 %column_and_feed.1 = bf16[512,768]{1,0:T(8,128)(2,1)} custom-call(s32[64,1]{1,0:T(8,128)} %copy.16.mask, bf16[512,768]{1,0:T(8,128)(2,1)} %bitcast.4, bf16[1,768]{1,0:T(2,128)(2,1)} %reshape.25.gc, bf16[1,768]{1,0:T(2,128)(2,1)} %reshape.26.gf, bf16[768,768]{1,0:T(8,128)(2,1)} %wq_h.3, bf16[768,768]{1,0:T(8,128)(2,1)} %wk_h.3, bf16[768,768]{1,0:T(8,128)(2,1)} %wv_h.3, ...), custom_call_target="tpu_custom_call" | custom-call | tf_op jit(solution)/shard_map/column_and_feed/pallas_call | solution.py:360
  158.9 2.1 %copy.18 = bf16[8,64,768]{2,1,0:T(8,128)(2,1)} copy(bf16[8,64,768]{2,1,0:T(8,128)(2,1)} %bitcast.5) | data formatting | bytes 1572864

commit v3 on v1

v3 whole, which is shorter than its diff:
```python
import jax
import jax.numpy as jnp
from jax import lax
from jax.experimental import pallas as pl
from jax.experimental.pallas import tpu as pltpu
from jax.sharding import PartitionSpec as P

D = 768
H = 12
DH = 64
FF = 3072
RL = 8
CL = 64
T = RL * CL
NS = 8
NZ = 4
NY = 4
NW = 4
HG = H // NY
BF = jnp.bfloat16
F32 = jnp.float32
MESH = pl.DeviceIdType.MESH
VMEM_LIMIT = 60 * 1024 * 1024


def norm(wide, gain):
    center = wide - jnp.mean(wide, axis=-1, keepdims=True)
    spread = jnp.mean(center * center, axis=-1, keepdims=True)
    return center * lax.rsqrt(spread + 1e-05) * gain


def dot(a, b, dims=((1,), (0,))):
    return lax.dot_general(a, b, (dims, ((), ())), preferred_element_type=F32)


def chunk(index, size):
    return pl.ds(pl.multiple_of(index * size, size), size)


class Load:
    def __init__(self, src, dst, sem):
        self.copy = pltpu.make_async_copy(src, dst, sem)
        self.copy.start()
        self.done = False

    def wait(self):
        if not self.done:
            self.copy.wait()
        self.done = True


class Push:
    def __init__(self, log, src, dst, sems, index, to):
        send, recv = sems
        self.copy = pltpu.make_async_remote_copy(
            src_ref=src, dst_ref=dst, send_sem=send.at[index], recv_sem=recv.at[index],
            device_id=to, device_id_type=MESH,
        )
        self.copy.start()
        self.got = self.left = False
        log.append(self)

    def recv(self):
        if not self.got:
            self.copy.wait_recv()
        self.got = True

    def sent(self):
        if not self.left:
            self.copy.wait_send()
        self.left = True


def finish(log, loads):
    for load in loads:
        load.wait()
    for push in log:
        push.recv()
    for push in log:
        push.sent()


def greet(peers):
    barrier = pltpu.get_barrier_semaphore()
    for peer in peers:
        pl.semaphore_signal(barrier, inc=1, device_id=peer, device_id_type=MESH)
    pl.semaphore_wait(barrier, len(peers))


def pair_lanes(a, b):
    low = lax.broadcasted_iota(jnp.int32, a.shape, 1) < DH
    return jnp.where(low, a, pltpu.roll(b, DH, 1)), jnp.where(low, pltpu.roll(a, DH, 1), b)


def layer_kernel(
    mask, x, gr, gc, gf, rq_h, rk_h, rv_h, ro_h, cq_h, ck_h, cv_h, co_h, up_h, dn_h, out,
    wrk, wrq, wrv, wro, wcq, wck, wcv, wco, up, dn,
    xn, acc, pk, qb, kb, vb, part, pb, rs, th, xs, xr, pw, mxs, mxr, cs, ci,
    xf, xo, cin, qc, kc, vc, hb, facc, cr, bias,
    lsem, ys, yr, fs, fr, zs, zr, hs, hr, as_, ar, ms, mr, cs_s, cs_r, os_, or_,
):
    s = lax.axis_index("seq")
    col = lax.axis_index("col")
    y, w = lax.div(col, NW), lax.rem(col, NW)
    xl, z = lax.div(s, NZ), lax.rem(s, NZ)
    yidx = [lax.rem(y + d, NY) for d in range(NY)]
    ydev = [(s, yidx[d] * NW + w) for d in range(NY)]
    zidx = [lax.rem(z + d, NZ) for d in range(NZ)]
    zdev = [(xl * NZ + zidx[d], col) for d in range(NZ)]
    xdev = ((1 - xl) * NZ + z, col)
    sidx = [lax.rem(s + d, NS) for d in range(NS)]
    sdev = [(sidx[d], col) for d in range(NS)]
    w_far = lax.rem(w + 2, NW)
    far = (s, y * NW + w_far)
    core = (s, y * NW + w + 1 - 2 * lax.rem(w, 2))

    pairs = (
        (rk_h, wrk), (rq_h, wrq), (rv_h, wrv), (ro_h, wro), (cq_h, wcq), (ck_h, wck), (cv_h, wcv),
        (co_h, wco), (up_h, up), (dn_h, dn),
    )
    loads = [Load(h, v, lsem.at[i]) for i, (h, v) in enumerate(pairs)]
    greet(ydev[1:] + [far, core] + sdev[1:])
    log = []

    def gain(ref):
        return ref[...].astype(F32).reshape(1, D)

    xn[...] = norm(x[...].astype(F32), gain(gr)).astype(BF)

    def project(kind, weight, load, into, base, masked=False):
        load.wait()
        acc[...] = dot(xn[...], weight[...])
        for p in range(RL // 2):
            for hp in range(H // 2):
                a = acc[2 * p * CL:(2 * p + 1) * CL, hp * 128:(hp + 1) * 128]
                b = acc[(2 * p + 1) * CL:(2 * p + 2) * CL, hp * 128:(hp + 1) * 128]
                if masked:
                    a = a * mask[s * RL + 2 * p].astype(F32)
                    b = b * mask[s * RL + 2 * p + 1].astype(F32)
                first, second = pair_lanes(a, b)
                pk[kind, 2 * hp, :, p * 128:(p + 1) * 128] = first.astype(BF)
                pk[kind, 2 * hp + 1, :, p * 128:(p + 1) * 128] = second.astype(BF)
        rows = chunk(base, CL)
        pushes = []
        for g in range(HG):
            pushes.append([
                Push(log, pk.at[kind, yidx[d] * HG + g], into.at[g, rows], (ys, yr), (kind, g, d - 1), ydev[d])
                for d in (2, 1, 3)
            ])
            into[g, rows, :] = pk[kind, y * HG + g]
        return pushes

    def spread(kind, ref, pushes, g):
        for p in pushes[g]:
            p.recv()
        block = ref.at[g, chunk(w, 256)]
        return (
            Push(log, block, block, (fs, fr), (kind, g, 0), far),
            Push(log, block, block, (fs, fr), (kind, g, 1), core),
        )

    def relay(kind, ref, pushes, g):
        pushes[0].recv()
        block = ref.at[g, chunk(w_far, 256)]
        last = Push(log, block, block, (fs, fr), (kind, g, 2), core)
        pushes[1].recv()
        return last

    def logits(g, last):
        for p in qy[g]:
            p.recv()
        last.recv()
        for j in range(4):
            part[g, :, j * 256:(j + 1) * 256] = dot(qb[g], kb[g, j * 256:(j + 1) * 256, :], ((1,), (1,)))
        shifted = part[g] - jnp.max(part[g], axis=-1, keepdims=True)
        part[g] = shifted
        pb[g] = shifted.astype(BF)
        return [
            Push(log, pb.at[g, chunk(zidx[d], 64)], rs.at[g, d - 1], (zs, zr), (g, d - 1), zdev[d]) for d in (2, 1, 3)
        ]

    def over_z(g, pushes):
        for p in pushes:
            p.recv()

        def half(index):
            total = part[g, chunk(z * 2 + index, 32), :]
            for d in range(NZ - 1):
                total = total + rs[g, d, chunk(index, 32), :].astype(F32)
            return total

        xs[g] = half(1 - xl)
        push = Push(log, xs.at[g], xr.at[g], (hs, hr), (g,), xdev)
        th[g] = half(xl)
        return push

    def soften(g, push):
        push.recv()
        total = (th[g] + xr[g]) * (1.0 / 64.0)
        e = jnp.exp(total - jnp.max(total, axis=-1, keepdims=True))
        rows = chunk(z * 2 + xl, 32)
        pw[g, rows, :] = (e / jnp.sum(e, axis=-1, keepdims=True)).astype(BF)
        block = pw.at[g, rows]
        return [Push(log, block, block, (as_, ar), (g, 0), xdev)] + [
            Push(log, block, block, (as_, ar), (g, d), zdev[d]) for d in (2, 1, 3)
        ]

    def onward(g, pushes):
        pushes[0].recv()
        block = pw.at[g, chunk(z * 2 + 1 - xl, 32)]
        return pushes + [Push(log, block, block, (as_, ar), (g, 3 + d), zdev[d]) for d in (2, 1, 3)]

    def mix(g, last, pushes):
        last.recv()
        for p in pushes:
            p.recv()
        mxs[g] = dot(pw[g], vb[g]).astype(BF)
        got = [
            Push(log, mxs.at[g, chunk(yidx[d], CL)], mxr.at[y * HG + g], (ms, mr), (g, d - 1), ydev[d])
            for d in (2, 1, 3)
        ]
        mxr[y * HG + g] = mxs[g, chunk(y, CL), :]
        return got

    own = w * NY + y
    ky = project(0, wrk, loads[0], kb, own)
    qy = project(1, wrq, loads[1], qb, y, masked=True)
    k0 = spread(0, kb, ky, 0)
    vy = project(2, wrv, loads[2], vb, own)
    k1 = spread(0, kb, ky, 1)
    k2 = spread(0, kb, ky, 2)
    k0 = relay(0, kb, k0, 0)
    z0 = logits(0, k0)
    k1 = relay(0, kb, k1, 1)
    z1 = logits(1, k1)
    x0 = over_z(0, z0)
    k2 = relay(0, kb, k2, 2)
    z2 = logits(2, k2)
    p0 = soften(0, x0)
    x1 = over_z(1, z1)
    v0 = spread(1, vb, vy, 0)
    p0 = onward(0, p0)
    p1 = soften(1, x1)
    v1 = spread(1, vb, vy, 1)
    x2 = over_z(2, z2)
    p1 = onward(1, p1)
    v2 = spread(1, vb, vy, 2)
    p2 = soften(2, x2)
    v0 = relay(1, vb, v0, 0)
    p2 = onward(2, p2)
    v1 = relay(1, vb, v1, 1)
    v2 = relay(1, vb, v2, 2)
    m = mix(0, v0, p0)
    m = m + mix(1, v1, p1)
    m = m + mix(2, v2, p2)
    for p in m:
        p.recv()
    for p in range(RL // 2):
        for hp in range(H // 2):
            a = mxr[2 * hp, :, p * 128:(p + 1) * 128].astype(F32)
            b = mxr[2 * hp + 1, :, p * 128:(p + 1) * 128].astype(F32)
            first, second = pair_lanes(a, b)
            xn[2 * p * CL:(2 * p + 1) * CL, hp * 128:(hp + 1) * 128] = first.astype(BF)
            xn[(2 * p + 1) * CL:(2 * p + 2) * CL, hp * 128:(hp + 1) * 128] = second.astype(BF)
    loads[3].wait()
    acc[...] = x[...].astype(F32) + dot(xn[...], wro[...])
    for t in range(NS):
        rows = [acc[r * CL + t * RL:r * CL + (t + 1) * RL, :] for r in range(RL)]
        cs[t] = jnp.concatenate(rows, axis=0).astype(BF)
    c_in = [Push(log, cs.at[sidx[d]], ci.at[s], (cs_s, cs_r), (d - 1,), sdev[d]) for d in range(1, NS)]
    ci[s] = cs[s]

    row = lax.broadcasted_iota(jnp.int32, (8, 128), 0)
    for t in range(NS):
        tile = jnp.zeros((8, 128), F32)
        for k in range(8):
            tile = jnp.where(row == k, mask[t * 8 + k].astype(F32), tile)
        bias[t * 8:(t + 1) * 8, :] = tile
    for p in c_in:
        p.recv()

    for j in range(D // 128):
        xf[j] = ci[:, :, j * 128:(j + 1) * 128].astype(F32).reshape(T, 128)
    for c in range(RL):
        xc = jnp.concatenate([xf[j, pl.ds(c, 64, stride=RL), :] for j in range(D // 128)], axis=1)
        xo[c * 64:(c + 1) * 64, :] = xc
        cin[c * 64:(c + 1) * 64, :] = norm(xc, gain(gc)).astype(BF)
    for load, weight, into in ((loads[4], wcq, qc), (loads[5], wck, kc), (loads[6], wcv, vc)):
        load.wait()
        into[...] = dot(cin[...], weight[...]).astype(BF)

    live = jnp.concatenate([bias[...], bias[...]], axis=1) > 0.5
    lane = lax.broadcasted_iota(jnp.int32, (1, 256), 1)
    pick = [((lane >= h * 64) & (lane < (h + 1) * 64)).astype(F32) for h in range(4)]

    @pl.loop(0, RL)
    def _(c):
        rows = chunk(c, 64)
        for g in range(3):
            lanes = slice(g * 256, (g + 1) * 256)
            q = qc[rows, lanes]
            qe = jnp.concatenate([q * pick[h].astype(BF) for h in range(4)], axis=0)
            st = dot(kc[rows, lanes], qe, ((1,), (1,))) * 0.125
            st = jnp.where(live, st, -1e30)
            e = jnp.exp(st - jnp.max(st, axis=0, keepdims=True))
            p = (e / jnp.sum(e, axis=0, keepdims=True)).astype(BF)
            res = dot(p, vc[rows, lanes], ((0,), (0,)))
            mixed = res[0:64] * pick[0]
            for h in range(1, 4):
                mixed = mixed + res[h * 64:(h + 1) * 64] * pick[h]
            cin[rows, lanes] = mixed.astype(BF)

    loads[7].wait()
    after = (xo[...] + dot(cin[...], wco[...])).astype(BF).astype(F32)
    facc[...] = after
    cin[...] = norm(after, gain(gf)).astype(BF)
    loads[8].wait()
    loads[9].wait()

    @pl.loop(0, FF // D)
    def _(n):
        part_n = chunk(n, D)
        h = dot(cin[...], up[:, part_n])
        hb[...] = (0.5 * h * (1.0 + lax.erf(h * 0.7071067811865476))).astype(BF)
        facc[...] += dot(hb[...], dn[part_n, :])
    for p in c_in:
        p.sent()
    for j in range(D // 128):
        lanes = slice(j * 128, (j + 1) * 128)
        for c in range(RL):
            xf[j, pl.ds(c, 64, stride=RL), :] = facc[c * 64:(c + 1) * 64, lanes]
        for t in range(NS):
            cs[t, :, lanes] = xf[j, t * 64:(t + 1) * 64, :].astype(BF)
    back = [Push(log, cs.at[sidx[d]], cr.at[s], (os_, or_), (d - 1,), sdev[d]) for d in range(1, NS)]
    cr[s] = cs[s]
    for p in back:
        p.recv()
    for m in range(NS // 2):
        a = cr[2 * m].astype(F32)
        b = cr[2 * m + 1].astype(F32)
        for r in range(RL):
            both = jnp.concatenate([a[r * 8:(r + 1) * 8], b[r * 8:(r + 1) * 8]], axis=0)
            out[r * CL + m * 16:r * CL + (m + 1) * 16, :] = both.astype(BF)
    finish(log, loads)


def vmem():
    return pl.BlockSpec(memory_space=pltpu.VMEM)


def hbm():
    return pl.BlockSpec(memory_space=pl.ANY)


def pairs_of(*shape):
    return [pltpu.SemaphoreType.DMA(shape)] * 2


def local(
    stream, row_mask, gain_row, row_query, row_key, row_value, row_output,
    gain_column, column_query, column_key, column_value, column_output,
    gain_feed, up_weight, down_weight,
):
    def bf(*shape):
        return pltpu.VMEM(shape, BF)

    def f32(*shape):
        return pltpu.VMEM(shape, F32)

    out = pl.pallas_call(
        layer_kernel,
        out_shape=jax.ShapeDtypeStruct((T, D), BF),
        in_specs=[pl.BlockSpec(memory_space=pltpu.SMEM)] + [vmem()] * 4 + [hbm()] * 10,
        out_specs=vmem(),
        scratch_shapes=[bf(D, D)] * 8 + [
            bf(D, FF), bf(FF, D),
            bf(T, D), f32(T, D), bf(3, H, CL, 512),
            bf(HG, 256, 512), bf(HG, 1024, 512), bf(HG, 1024, 512),
            f32(HG, 256, 1024), bf(HG, 256, 1024), bf(HG, NZ - 1, 64, 1024),
            f32(HG, 32, 1024), f32(HG, 32, 1024), f32(HG, 32, 1024),
            bf(HG, 256, 1024), bf(HG, 256, 512), bf(H, CL, 512),
            bf(NS, 64, D), bf(NS, 64, D),
            f32(D // 128, T, 128), f32(T, D), bf(T, D), bf(T, D), bf(T, D), bf(T, D), bf(T, D),
            f32(T, D), bf(NS, 64, D), f32(64, 128),
            pltpu.SemaphoreType.DMA((10,)),
        ] + pairs_of(3, HG, NY - 1) + pairs_of(2, HG, 3) + pairs_of(HG, NZ - 1) + pairs_of(HG)
        + pairs_of(HG, 7) + pairs_of(HG, NY - 1) + pairs_of(NS - 1) + pairs_of(NS - 1),
        compiler_params=pltpu.CompilerParams(
            collective_id=0, has_side_effects=True, vmem_limit_bytes=VMEM_LIMIT
        ),
        name="layer",
    )(
        row_mask, stream.reshape(T, D), gain_row, gain_column, gain_feed,
        row_query, row_key, row_value, row_output,
        column_query, column_key, column_value, column_output, up_weight, down_weight,
    )
    return out.reshape(RL, CL, D)


def solution(mesh):
    return jax.shard_map(
        local,
        mesh=mesh,
        in_specs=(P("seq", "col", None),) + (P(),) * 14,
        out_specs=P("seq", "col", None),
        check_vma=False,
    )
```

time: 362 us -> 128 us (0.35); the launches traced: 355 us -> 126 us
  Pallas kernels: 0 us -> 124 us
  waiting for transfers between devices: 121 us -> 0 us
  blocking collectives: 82.8 us -> 0 us
  local copies, waits for them, and re-layouts: 69 us -> 2.06 us
  matrix products: 55.4 us -> 0 us
  between operations: 13.6 us -> 0.01 us
  other arithmetic: 9.8 us -> 0 us
  starting transfers between devices: 4.06 us -> 0 us
    pallas_call x0 -> x1, Pallas kernels: none -> 124 us  [local(): pl.pallas_call(layer_kernel, out_shape=jax.ShapeDtypeStruct((T, D), BF),...]
    all_gather x3 -> x0, waiting for transfers between devices: 88.6 us -> none  [the longest x1 37.9 us: local(): vv = lax.all_gather(v, 'col', axis=0, axis_index_groups=W_GROUPS)]
    all_to_all x5 -> x0, blocking collectives: 82.8 us -> none  [the longest x3 55.2 us: to_heads(): lax.all_to_all(out, 'col', 0, 0, axis_index_groups=Y_GROUPS, tiled=True)]
    dot_general x13 -> x0, matrix products: 55.4 us -> none  [the longest x9 40.9 us: dot(): return jnp.dot(a, b, preferred_element_type=jnp.float32)]
    reshape x16 -> x0, local copies, waits for them, and re-layouts: 36.4 us -> none  [the longest x1 7.31 us: local(): part = part.reshape(hg, 4 * cols, 16 * cols)]
    reduce_scatter x1 -> x0, waiting for transfers between devices: 22.5 us -> none  [local(): tied = lax.psum_scatter(part, 'seq', scatter_dimension=1, tiled=True)]
    all_gather x2 -> x0, local copies, waits for them, and re-layouts: 15.8 us -> none  [the longest x1 7.89 us: local(): kk = lax.all_gather(k, 'col', axis=0, axis_index_groups=W_GROUPS)]
    all_to_all x1 -> x0, waiting for transfers between devices: 9.35 us -> none  [local(): moved = lax.all_to_all(moved, 'seq', 0, 0, tiled=True)]
  transfers between devices with their start and end apart: 5 -> 0, of which waited for: 5 -> 0; matrix products, arithmetic and copies ran while one was open for 5% -> 0% of each run, Pallas kernels for 0% -> 0%
where the time goes in v3:
time: 128 us; the launch traced here: 126 us
  Pallas kernels  124 us (97%)
  local copies, waits for them, and re-layouts  2.06 us (2%)
    pallas_call x1, Pallas kernels, local(): pl.pallas_call(layer_kernel, out_shape=jax.ShapeDtypeStruct((T, D), BF),...  124 us

profile of v3, /device:TPU:8, one launch (start us, length us, event | category | flops | bytes accessed | tf_op | source)
XLA Modules:
  0.0 125.9 jit_solution(16488549876117954908)
XLA Ops:
  0.0 123.9 %layer.1 = bf16[512,768]{1,0:T(8,128)(2,1)} custom-call(s32[64]{0:T(128)} %mask.1, bf16[512,768]{1,0:T(8,128)(2,1)} %bitcast.3, bf16[768]{0:T(1024)(128)(2,1)} %gr.1, bf16[768]{0:T(1024)(128)(2,1)} %gc.1, bf16[768]{0:T(1024)(128)(2,1)} %gf.1, bf16[768,768]{1,0:T(8,128)(2,1)} %rq_h.1, bf16[768,768]{1,0:T(8,128)(2,1)} %rk_h.1, bf16[768,768]{1,0:T(8,128)(2,1)} %rv_h.1, ...), custom_call_target="tpu_custom_call" | custom-call | tf_op jit(solution)/shard_map/layer/pallas_call | solution.py:370
  123.9 2.1 %copy.17 = bf16[8,64,768]{2,1,0:T(8,128)(2,1)} copy(bf16[8,64,768]{2,1,0:T(8,128)(2,1)} %bitcast.2) | data formatting | bytes 1572864

commit v4 on v3

--- a/solution.py
+++ b/solution.py
@@ -80,13 +80,6 @@
         push.sent()
 
 
-def greet(peers):
-    barrier = pltpu.get_barrier_semaphore()
-    for peer in peers:
-        pl.semaphore_signal(barrier, inc=1, device_id=peer, device_id_type=MESH)
-    pl.semaphore_wait(barrier, len(peers))
-
-
 def pair_lanes(a, b):
     low = lax.broadcasted_iota(jnp.int32, a.shape, 1) < DH
     return jnp.where(low, a, pltpu.roll(b, DH, 1)), jnp.where(low, pltpu.roll(a, DH, 1), b)
@@ -96,7 +89,7 @@
     mask, x, gr, gc, gf, rq_h, rk_h, rv_h, ro_h, cq_h, ck_h, cv_h, co_h, up_h, dn_h, out,
     wrk, wrq, wrv, wro, wcq, wck, wcv, wco, up, dn,
     xn, acc, pk, qb, kb, vb, part, pb, rs, th, xs, xr, pw, mxs, mxr, cs, ci,
-    xf, xo, cin, qc, kc, vc, hb, facc, cr, bias,
+    xf, xo, cin, qc, kc, vc, hb, facc, co, cr, bias,
     lsem, ys, yr, fs, fr, zs, zr, hs, hr, as_, ar, ms, mr, cs_s, cs_r, os_, or_,
 ):
     s = lax.axis_index("seq")
@@ -119,7 +112,10 @@
         (co_h, wco), (up_h, up), (dn_h, dn),
     )
     loads = [Load(h, v, lsem.at[i]) for i, (h, v) in enumerate(pairs)]
-    greet(ydev[1:] + [far, core] + sdev[1:])
+    barrier = pltpu.get_barrier_semaphore()
+    peers = ydev[1:] + [far, core] + sdev[1:]
+    for peer in peers:
+        pl.semaphore_signal(barrier, inc=1, device_id=peer, device_id_type=MESH)
     log = []
 
     def gain(ref):
@@ -127,7 +123,7 @@
 
     xn[...] = norm(x[...].astype(F32), gain(gr)).astype(BF)
 
-    def project(kind, weight, load, into, base, masked=False):
+    def project(kind, weight, load, masked=False):
         load.wait()
         acc[...] = dot(xn[...], weight[...])
         for p in range(RL // 2):
@@ -140,14 +136,14 @@
                 first, second = pair_lanes(a, b)
                 pk[kind, 2 * hp, :, p * 128:(p + 1) * 128] = first.astype(BF)
                 pk[kind, 2 * hp + 1, :, p * 128:(p + 1) * 128] = second.astype(BF)
+
+    def over_y(kind, into, base, g):
         rows = chunk(base, CL)
-        pushes = []
-        for g in range(HG):
-            pushes.append([
-                Push(log, pk.at[kind, yidx[d] * HG + g], into.at[g, rows], (ys, yr), (kind, g, d - 1), ydev[d])
-                for d in (2, 1, 3)
-            ])
-            into[g, rows, :] = pk[kind, y * HG + g]
+        pushes = [
+            Push(log, pk.at[kind, yidx[d] * HG + g], into.at[g, rows], (ys, yr), (kind, g, d - 1), ydev[d])
+            for d in (2, 1, 3)
+        ]
+        into[g, rows, :] = pk[kind, y * HG + g]
         return pushes
 
     def spread(kind, ref, pushes, g):
@@ -223,32 +219,41 @@
         return got
 
     own = w * NY + y
-    ky = project(0, wrk, loads[0], kb, own)
-    qy = project(1, wrq, loads[1], qb, y, masked=True)
+    ky, qy, vy = [None] * HG, [None] * HG, [None] * HG
+    project(0, wrk, loads[0])
+    pl.semaphore_wait(barrier, len(peers))
+    ky[0] = over_y(0, kb, own, 0)
+    project(1, wrq, loads[1], masked=True)
+    qy[0] = over_y(1, qb, y, 0)
+    for g in range(1, HG):
+        ky[g] = over_y(0, kb, own, g)
+        qy[g] = over_y(1, qb, y, g)
     k0 = spread(0, kb, ky, 0)
-    vy = project(2, wrv, loads[2], vb, own)
+    project(2, wrv, loads[2])
+    for g in range(HG):
+        vy[g] = over_y(2, vb, own, g)
     k1 = spread(0, kb, ky, 1)
-    k2 = spread(0, kb, ky, 2)
     k0 = relay(0, kb, k0, 0)
     z0 = logits(0, k0)
+    k2 = spread(0, kb, ky, 2)
     k1 = relay(0, kb, k1, 1)
     z1 = logits(1, k1)
     x0 = over_z(0, z0)
     k2 = relay(0, kb, k2, 2)
     z2 = logits(2, k2)
+    v0 = spread(1, vb, vy, 0)
     p0 = soften(0, x0)
+    v1 = spread(1, vb, vy, 1)
     x1 = over_z(1, z1)
-    v0 = spread(1, vb, vy, 0)
+    v2 = spread(1, vb, vy, 2)
     p0 = onward(0, p0)
     p1 = soften(1, x1)
-    v1 = spread(1, vb, vy, 1)
     x2 = over_z(2, z2)
     p1 = onward(1, p1)
-    v2 = spread(1, vb, vy, 2)
+    v0 = relay(1, vb, v0, 0)
     p2 = soften(2, x2)
-    v0 = relay(1, vb, v0, 0)
+    v1 = relay(1, vb, v1, 1)
     p2 = onward(2, p2)
-    v1 = relay(1, vb, v1, 1)
     v2 = relay(1, vb, v2, 2)
     m = mix(0, v0, p0)
     m = m + mix(1, v1, p1)
@@ -263,12 +268,23 @@
             xn[2 * p * CL:(2 * p + 1) * CL, hp * 128:(hp + 1) * 128] = first.astype(BF)
             xn[(2 * p + 1) * CL:(2 * p + 2) * CL, hp * 128:(hp + 1) * 128] = second.astype(BF)
     loads[3].wait()
-    acc[...] = x[...].astype(F32) + dot(xn[...], wro[...])
-    for t in range(NS):
-        rows = [acc[r * CL + t * RL:r * CL + (t + 1) * RL, :] for r in range(RL)]
-        cs[t] = jnp.concatenate(rows, axis=0).astype(BF)
-    c_in = [Push(log, cs.at[sidx[d]], ci.at[s], (cs_s, cs_r), (d - 1,), sdev[d]) for d in range(1, NS)]
-    ci[s] = cs[s]
+    for n in range(D // 256):
+        wide = dot(xn[...], wro[:, n * 256:(n + 1) * 256])
+        for j in (2 * n, 2 * n + 1):
+            lanes = slice(j * 128, (j + 1) * 128)
+            xf[j] = x[:, lanes].astype(F32) + wide[:, (j - 2 * n) * 128:(j - 2 * n + 1) * 128]
+
+    c_in = []
+    for half in range(2):
+        for t in range(NS):
+            for j in range(D // 128):
+                tiles = [xf[j, pl.ds(t * 8 + half * 4 + k, RL, stride=CL), :] for k in range(4)]
+                cs[half, t, :, j * 128:(j + 1) * 128] = jnp.concatenate(tiles, axis=0).astype(BF)
+        c_in.append([
+            Push(log, cs.at[half, sidx[d]], ci.at[half, s], (cs_s, cs_r), (half, d - 1), sdev[d])
+            for d in (2, 6, 1, 3, 5, 7, 4)
+        ])
+        ci[half, s] = cs[half, s]
 
     row = lax.broadcasted_iota(jnp.int32, (8, 128), 0)
     for t in range(NS):
@@ -276,71 +292,79 @@
         for k in range(8):
             tile = jnp.where(row == k, mask[t * 8 + k].astype(F32), tile)
         bias[t * 8:(t + 1) * 8, :] = tile
-    for p in c_in:
-        p.recv()
-
-    for j in range(D // 128):
-        xf[j] = ci[:, :, j * 128:(j + 1) * 128].astype(F32).reshape(T, 128)
-    for c in range(RL):
-        xc = jnp.concatenate([xf[j, pl.ds(c, 64, stride=RL), :] for j in range(D // 128)], axis=1)
-        xo[c * 64:(c + 1) * 64, :] = xc
-        cin[c * 64:(c + 1) * 64, :] = norm(xc, gain(gc)).astype(BF)
-    for load, weight, into in ((loads[4], wcq, qc), (loads[5], wck, kc), (loads[6], wcv, vc)):
-        load.wait()
-        into[...] = dot(cin[...], weight[...]).astype(BF)
-
     live = jnp.concatenate([bias[...], bias[...]], axis=1) > 0.5
     lane = lax.broadcasted_iota(jnp.int32, (1, 256), 1)
     pick = [((lane >= h * 64) & (lane < (h + 1) * 64)).astype(F32) for h in range(4)]
 
-    @pl.loop(0, RL)
-    def _(c):
-        rows = chunk(c, 64)
-        for g in range(3):
-            lanes = slice(g * 256, (g + 1) * 256)
+    def attend(tiles):
+        scores = []
+        for rows, lanes in tiles:
             q = qc[rows, lanes]
-            qe = jnp.concatenate([q * pick[h].astype(BF) for h in range(4)], axis=0)
-            st = dot(kc[rows, lanes], qe, ((1,), (1,))) * 0.125
-            st = jnp.where(live, st, -1e30)
+            wide = jnp.concatenate([q * pick[h].astype(BF) for h in range(4)], axis=0)
+            scores.append(dot(kc[rows, lanes], wide, ((1,), (1,))))
+        weights = []
+        for st in scores:
+            st = jnp.where(live, st * 0.125, -1e30)
             e = jnp.exp(st - jnp.max(st, axis=0, keepdims=True))
-            p = (e / jnp.sum(e, axis=0, keepdims=True)).astype(BF)
+            weights.append((e / jnp.sum(e, axis=0, keepdims=True)).astype(BF))
+        for (rows, lanes), p in zip(tiles, weights):
             res = dot(p, vc[rows, lanes], ((0,), (0,)))
             mixed = res[0:64] * pick[0]
             for h in range(1, 4):
                 mixed = mixed + res[h * 64:(h + 1) * 64] * pick[h]
             cin[rows, lanes] = mixed.astype(BF)
 
-    loads[7].wait()
-    after = (xo[...] + dot(cin[...], wco[...])).astype(BF).astype(F32)
-    facc[...] = after
-    cin[...] = norm(after, gain(gf)).astype(BF)
-    loads[8].wait()
-    loads[9].wait()
-
-    @pl.loop(0, FF // D)
-    def _(n):
-        part_n = chunk(n, D)
-        h = dot(cin[...], up[:, part_n])
-        hb[...] = (0.5 * h * (1.0 + lax.erf(h * 0.7071067811865476))).astype(BF)
-        facc[...] += dot(hb[...], dn[part_n, :])
-    for p in c_in:
-        p.sent()
+    back = []
+    for half in range(2):
+        for p in c_in[half]:
+            p.recv()
+        for k in range(4):
+            xo[k * 64:(k + 1) * 64, :] = jnp.concatenate(
+                [ci[half, t].astype(F32)[k * 8:(k + 1) * 8] for t in range(NS)], axis=0
+            )
+        cin[...] = norm(xo[...], gain(gc)).astype(BF)
+        for load, weight, into in ((loads[4], wcq, qc), (loads[5], wck, kc), (loads[6], wcv, vc)):
+            load.wait()
+            into[...] = dot(cin[...], weight[...]).astype(BF)
+
+        @pl.loop(0, 2)
+        def _(step):
+            attend([
+                (chunk(step * 2 + c, 64), slice(g * 256, (g + 1) * 256)) for c in range(2) for g in range(3)
+            ])
+
+        loads[7].wait()
+        after = (xo[...] + dot(cin[...], wco[...])).astype(BF).astype(F32)
+        facc[...] = after
+        cin[...] = norm(after, gain(gf)).astype(BF)
+        loads[8].wait()
+        loads[9].wait()
+
+        @pl.loop(0, FF // D)
+        def _(n):
+            part_n = chunk(n, D)
+            h = dot(cin[...], up[:, part_n])
+            hb[...] = (0.5 * h * (1.0 + lax.erf(h * 0.7071067811865476))).astype(BF)
+            facc[...] += dot(hb[...], dn[part_n, :])
+
+        for t in range(NS):
+            tiles = [facc[k * 64 + t * 8:k * 64 + (t + 1) * 8, :] for k in range(4)]
+            co[half, t] = jnp.concatenate(tiles, axis=0).astype(BF)
+        back.append([
+            Push(log, co.at[half, sidx[d]], cr.at[half, s], (os_, or_), (half, d - 1), sdev[d])
+            for d in (2, 6, 1, 3, 5, 7, 4)
+        ])
+        cr[half, s] = co[half, s]
+    for half in range(2):
+        for p in back[half]:
+            p.recv()
+        for t in range(NS):
+            for j in range(D // 128):
+                wide = cr[half, t, :, j * 128:(j + 1) * 128].astype(F32)
+                for k in range(4):
+                    xf[j, pl.ds(t * 8 + half * 4 + k, RL, stride=CL), :] = wide[k * 8:(k + 1) * 8]
     for j in range(D // 128):
-        lanes = slice(j * 128, (j + 1) * 128)
-        for c in range(RL):
-            xf[j, pl.ds(c, 64, stride=RL), :] = facc[c * 64:(c + 1) * 64, lanes]
-        for t in range(NS):
-            cs[t, :, lanes] = xf[j, t * 64:(t + 1) * 64, :].astype(BF)
-    back = [Push(log, cs.at[sidx[d]], cr.at[s], (os_, or_), (d - 1,), sdev[d]) for d in range(1, NS)]
-    cr[s] = cs[s]
-    for p in back:
-        p.recv()
-    for m in range(NS // 2):
-        a = cr[2 * m].astype(F32)
-        b = cr[2 * m + 1].astype(F32)
-        for r in range(RL):
-            both = jnp.concatenate([a[r * 8:(r + 1) * 8], b[r * 8:(r + 1) * 8]], axis=0)
-            out[r * CL + m * 16:r * CL + (m + 1) * 16, :] = both.astype(BF)
+        out[:, j * 128:(j + 1) * 128] = xf[j].astype(BF)
     finish(log, loads)
 
 
@@ -379,12 +403,12 @@
             f32(HG, 256, 1024), bf(HG, 256, 1024), bf(HG, NZ - 1, 64, 1024),
             f32(HG, 32, 1024), f32(HG, 32, 1024), f32(HG, 32, 1024),
             bf(HG, 256, 1024), bf(HG, 256, 512), bf(H, CL, 512),
-            bf(NS, 64, D), bf(NS, 64, D),
-            f32(D // 128, T, 128), f32(T, D), bf(T, D), bf(T, D), bf(T, D), bf(T, D), bf(T, D),
-            f32(T, D), bf(NS, 64, D), f32(64, 128),
+            bf(2, NS, 32, D), bf(2, NS, 32, D),
+            f32(D // 128, T, 128), f32(256, D), bf(256, D), bf(256, D), bf(256, D), bf(256, D), bf(256, D),
+            f32(256, D), bf(2, NS, 32, D), bf(2, NS, 32, D), f32(64, 128),
             pltpu.SemaphoreType.DMA((10,)),
         ] + pairs_of(3, HG, NY - 1) + pairs_of(2, HG, 3) + pairs_of(HG, NZ - 1) + pairs_of(HG)
-        + pairs_of(HG, 7) + pairs_of(HG, NY - 1) + pairs_of(NS - 1) + pairs_of(NS - 1),
+        + pairs_of(HG, 7) + pairs_of(HG, NY - 1) + pairs_of(2, NS - 1) + pairs_of(2, NS - 1),
         compiler_params=pltpu.CompilerParams(
             collective_id=0, has_side_effects=True, vmem_limit_bytes=VMEM_LIMIT
         ),

time: 128 us -> 112 us (0.88); the launches traced: 126 us -> 111 us
  Pallas kernels: 124 us -> 109 us
    pallas_call x1, Pallas kernels: 124 us -> 109 us  [local(): pl.pallas_call(layer_kernel, out_shape=jax.ShapeDtypeStruct((T, D), BF),...]
where the time goes in v4:
time: 112 us; the launch traced here: 111 us
  Pallas kernels  109 us (97%)
  local copies, waits for them, and re-layouts  2.06 us (2%)
    pallas_call x1, Pallas kernels, local(): pl.pallas_call(layer_kernel, out_shape=jax.ShapeDtypeStruct((T, D), BF),...  109 us

profile of v4, /device:TPU:8, one launch (start us, length us, event | category | flops | bytes accessed | tf_op | source)
XLA Modules:
  0.0 111.5 jit_solution(6120017791302376754)
XLA Ops:
  0.0 109.4 %layer.1 = bf16[512,768]{1,0:T(8,128)(2,1)} custom-call(s32[64]{0:T(128)} %mask.1, bf16[512,768]{1,0:T(8,128)(2,1)} %bitcast.3, bf16[768]{0:T(1024)(128)(2,1)} %gr.1, bf16[768]{0:T(1024)(128)(2,1)} %gc.1, bf16[768]{0:T(1024)(128)(2,1)} %gf.1, bf16[768,768]{1,0:T(8,128)(2,1)} %rq_h.1, bf16[768,768]{1,0:T(8,128)(2,1)} %rk_h.1, bf16[768,768]{1,0:T(8,128)(2,1)} %rv_h.1, ...), custom_call_target="tpu_custom_call" | custom-call | tf_op jit(solution)/shard_map/layer/pallas_call | solution.py:394
  109.4 2.1 %copy.17 = bf16[8,64,768]{2,1,0:T(8,128)(2,1)} copy(bf16[8,64,768]{2,1,0:T(8,128)(2,1)} %bitcast.2) | data formatting | bytes 1572864

commit v5 on v4

--- a/solution.py
+++ b/solution.py
@@ -167,8 +167,12 @@
             p.recv()
         last.recv()
         for j in range(4):
-            part[g, :, j * 256:(j + 1) * 256] = dot(qb[g], kb[g, j * 256:(j + 1) * 256, :], ((1,), (1,)))
-        shifted = part[g] - jnp.max(part[g], axis=-1, keepdims=True)
+            block = dot(qb[g], kb[g, j * 256:(j + 1) * 256, :], ((1,), (1,)))
+            part[g, :, j * 256:(j + 1) * 256] = block * (1.0 / 64.0)
+        raw = part[g]
+        e = jnp.exp(raw - jnp.max(raw, axis=-1, keepdims=True))
+        center = jnp.sum(e * raw, axis=-1, keepdims=True) / jnp.sum(e, axis=-1, keepdims=True)
+        shifted = raw - center
         part[g] = shifted
         pb[g] = shifted.astype(BF)
         return [
@@ -178,33 +182,21 @@
     def over_z(g, pushes):
         for p in pushes:
             p.recv()
-
-        def half(index):
-            total = part[g, chunk(z * 2 + index, 32), :]
-            for d in range(NZ - 1):
-                total = total + rs[g, d, chunk(index, 32), :].astype(F32)
-            return total
-
-        xs[g] = half(1 - xl)
-        push = Push(log, xs.at[g], xr.at[g], (hs, hr), (g,), xdev)
-        th[g] = half(xl)
-        return push
+        total = part[g, chunk(z, 64), :]
+        for d in range(NZ - 1):
+            total = total + rs[g, d].astype(F32)
+        th[g] = total
+        xs[g] = total.astype(BF)
+        return Push(log, xs.at[g], xr.at[g], (hs, hr), (g,), xdev)
 
     def soften(g, push):
         push.recv()
-        total = (th[g] + xr[g]) * (1.0 / 64.0)
+        total = th[g] + xr[g].astype(F32)
         e = jnp.exp(total - jnp.max(total, axis=-1, keepdims=True))
-        rows = chunk(z * 2 + xl, 32)
+        rows = chunk(z, 64)
         pw[g, rows, :] = (e / jnp.sum(e, axis=-1, keepdims=True)).astype(BF)
         block = pw.at[g, rows]
-        return [Push(log, block, block, (as_, ar), (g, 0), xdev)] + [
-            Push(log, block, block, (as_, ar), (g, d), zdev[d]) for d in (2, 1, 3)
-        ]
-
-    def onward(g, pushes):
-        pushes[0].recv()
-        block = pw.at[g, chunk(z * 2 + 1 - xl, 32)]
-        return pushes + [Push(log, block, block, (as_, ar), (g, 3 + d), zdev[d]) for d in (2, 1, 3)]
+        return [Push(log, block, block, (as_, ar), (g, d - 1), zdev[d]) for d in (2, 1, 3)]
 
     def mix(g, last, pushes):
         last.recv()
@@ -241,22 +233,19 @@
     x0 = over_z(0, z0)
     k2 = relay(0, kb, k2, 2)
     z2 = logits(2, k2)
+    x1 = over_z(1, z1)
     v0 = spread(1, vb, vy, 0)
     p0 = soften(0, x0)
-    v1 = spread(1, vb, vy, 1)
-    x1 = over_z(1, z1)
-    v2 = spread(1, vb, vy, 2)
-    p0 = onward(0, p0)
     p1 = soften(1, x1)
     x2 = over_z(2, z2)
-    p1 = onward(1, p1)
+    v1 = spread(1, vb, vy, 1)
+    v2 = spread(1, vb, vy, 2)
+    p2 = soften(2, x2)
     v0 = relay(1, vb, v0, 0)
-    p2 = soften(2, x2)
+    m = mix(0, v0, p0)
     v1 = relay(1, vb, v1, 1)
-    p2 = onward(2, p2)
+    m = m + mix(1, v1, p1)
     v2 = relay(1, vb, v2, 2)
-    m = mix(0, v0, p0)
-    m = m + mix(1, v1, p1)
     m = m + mix(2, v2, p2)
     for p in m:
         p.recv()
@@ -401,14 +390,14 @@
             bf(T, D), f32(T, D), bf(3, H, CL, 512),
             bf(HG, 256, 512), bf(HG, 1024, 512), bf(HG, 1024, 512),
             f32(HG, 256, 1024), bf(HG, 256, 1024), bf(HG, NZ - 1, 64, 1024),
-            f32(HG, 32, 1024), f32(HG, 32, 1024), f32(HG, 32, 1024),
+            f32(HG, 64, 1024), bf(HG, 64, 1024), bf(HG, 64, 1024),
             bf(HG, 256, 1024), bf(HG, 256, 512), bf(H, CL, 512),
             bf(2, NS, 32, D), bf(2, NS, 32, D),
             f32(D // 128, T, 128), f32(256, D), bf(256, D), bf(256, D), bf(256, D), bf(256, D), bf(256, D),
             f32(256, D), bf(2, NS, 32, D), bf(2, NS, 32, D), f32(64, 128),
             pltpu.SemaphoreType.DMA((10,)),
         ] + pairs_of(3, HG, NY - 1) + pairs_of(2, HG, 3) + pairs_of(HG, NZ - 1) + pairs_of(HG)
-        + pairs_of(HG, 7) + pairs_of(HG, NY - 1) + pairs_of(2, NS - 1) + pairs_of(2, NS - 1),
+        + pairs_of(HG, NZ - 1) + pairs_of(HG, NY - 1) + pairs_of(2, NS - 1) + pairs_of(2, NS - 1),
         compiler_params=pltpu.CompilerParams(
             collective_id=0, has_side_effects=True, vmem_limit_bytes=VMEM_LIMIT
         ),

time: 112 us -> 106 us (0.946); the launches traced: 111 us -> 104 us
  Pallas kernels: 109 us -> 102 us
    pallas_call x1, Pallas kernels: 109 us -> 102 us  [local(): pl.pallas_call(layer_kernel, out_shape=jax.ShapeDtypeStruct((T, D), BF),...]
where the time goes in v5:
time: 106 us; the launch traced here: 104 us
  Pallas kernels  102 us (96%)
  local copies, waits for them, and re-layouts  2.06 us (2%)
    pallas_call x1, Pallas kernels, local(): pl.pallas_call(layer_kernel, out_shape=jax.ShapeDtypeStruct((T, D), BF),...  102 us

profile of v5, /device:TPU:8, one launch (start us, length us, event | category | flops | bytes accessed | tf_op | source)
XLA Modules:
  0.0 104.2 jit_solution(8484072347368660325)
XLA Ops:
  0.0 102.1 %layer.1 = bf16[512,768]{1,0:T(8,128)(2,1)} custom-call(s32[64]{0:T(128)} %mask.1, bf16[512,768]{1,0:T(8,128)(2,1)} %bitcast.3, bf16[768]{0:T(1024)(128)(2,1)} %gr.1, bf16[768]{0:T(1024)(128)(2,1)} %gc.1, bf16[768]{0:T(1024)(128)(2,1)} %gf.1, bf16[768,768]{1,0:T(8,128)(2,1)} %rq_h.1, bf16[768,768]{1,0:T(8,128)(2,1)} %rk_h.1, bf16[768,768]{1,0:T(8,128)(2,1)} %rv_h.1, ...), custom_call_target="tpu_custom_call" | custom-call | tf_op jit(solution)/shard_map/layer/pallas_call | solution.py:383
  102.1 2.1 %copy.17 = bf16[8,64,768]{2,1,0:T(8,128)(2,1)} copy(bf16[8,64,768]{2,1,0:T(8,128)(2,1)} %bitcast.2) | data formatting | bytes 1572864

commit v6 on v5

--- a/solution.py
+++ b/solution.py
@@ -90,7 +90,7 @@
     wrk, wrq, wrv, wro, wcq, wck, wcv, wco, up, dn,
     xn, acc, pk, qb, kb, vb, part, pb, rs, th, xs, xr, pw, mxs, mxr, cs, ci,
     xf, xo, cin, qc, kc, vc, hb, facc, co, cr, bias,
-    lsem, ys, yr, fs, fr, zs, zr, hs, hr, as_, ar, ms, mr, cs_s, cs_r, os_, or_,
+    lsem, ys, yr, fs, fr, ps, pr, zs, zr, hs, hr, as_, ar, ms, mr, cs_s, cs_r, os_, or_,
 ):
     s = lax.axis_index("seq")
     col = lax.axis_index("col")
@@ -155,6 +155,22 @@
             Push(log, block, block, (fs, fr), (kind, g, 1), core),
         )
 
+    def piece(index, i):
+        block = kb.at[0, chunk(w * NY + index, CL)]
+        return (
+            Push(log, block, block, (ps, pr), (0, i), far),
+            Push(log, block, block, (ps, pr), (1, i), core),
+        )
+
+    def join(pieces):
+        for a, b in pieces:
+            a.recv()
+        block = kb.at[0, chunk(w_far, 256)]
+        last = Push(log, block, block, (fs, fr), (0, 0, 2), core)
+        for a, b in pieces:
+            b.recv()
+        return last
+
     def relay(kind, ref, pushes, g):
         pushes[0].recv()
         block = ref.at[g, chunk(w_far, 256)]
@@ -196,7 +212,19 @@
         rows = chunk(z, 64)
         pw[g, rows, :] = (e / jnp.sum(e, axis=-1, keepdims=True)).astype(BF)
         block = pw.at[g, rows]
-        return [Push(log, block, block, (as_, ar), (g, d - 1), zdev[d]) for d in (2, 1, 3)]
+        return [
+            Push(log, block, block, (as_, ar), (g, 0), zdev[1]),
+            Push(log, block, block, (as_, ar), (g, 1), zdev[3]),
+        ]
+
+    def onward(g, pushes):
+        pushes[0].recv()
+        first = pw.at[g, chunk(zidx[3] * 2, 32)]
+        a = Push(log, first, first, (as_, ar), (g, 2), zdev[1])
+        pushes[1].recv()
+        second = pw.at[g, chunk(zidx[1] * 2 + 1, 32)]
+        b = Push(log, second, second, (as_, ar), (g, 3), zdev[3])
+        return [a, b]
 
     def mix(g, last, pushes):
         last.recv()
@@ -215,34 +243,41 @@
     project(0, wrk, loads[0])
     pl.semaphore_wait(barrier, len(peers))
     ky[0] = over_y(0, kb, own, 0)
+    k0 = [piece(y, 0)]
     project(1, wrq, loads[1], masked=True)
+    ky[1] = over_y(0, kb, own, 1)
     qy[0] = over_y(1, qb, y, 0)
-    for g in range(1, HG):
-        ky[g] = over_y(0, kb, own, g)
-        qy[g] = over_y(1, qb, y, g)
-    k0 = spread(0, kb, ky, 0)
+    ky[2] = over_y(0, kb, own, 2)
+    qy[1] = over_y(1, qb, y, 1)
+    qy[2] = over_y(1, qb, y, 2)
+    for push, d in ((ky[0][1], 3), (ky[0][2], 1), (ky[0][0], 2)):
+        push.recv()
+        k0.append(piece(yidx[d], d))
     project(2, wrv, loads[2])
     for g in range(HG):
         vy[g] = over_y(2, vb, own, g)
     k1 = spread(0, kb, ky, 1)
-    k0 = relay(0, kb, k0, 0)
+    k0 = join(k0)
     z0 = logits(0, k0)
     k2 = spread(0, kb, ky, 2)
     k1 = relay(0, kb, k1, 1)
     z1 = logits(1, k1)
     x0 = over_z(0, z0)
     k2 = relay(0, kb, k2, 2)
+    v0 = spread(1, vb, vy, 0)
     z2 = logits(2, k2)
+    p0 = soften(0, x0)
     x1 = over_z(1, z1)
-    v0 = spread(1, vb, vy, 0)
-    p0 = soften(0, x0)
-    p1 = soften(1, x1)
     x2 = over_z(2, z2)
     v1 = spread(1, vb, vy, 1)
     v2 = spread(1, vb, vy, 2)
+    p1 = soften(1, x1)
+    p0 = onward(0, p0)
+    v0 = relay(1, vb, v0, 0)
     p2 = soften(2, x2)
-    v0 = relay(1, vb, v0, 0)
     m = mix(0, v0, p0)
+    p1 = onward(1, p1)
+    p2 = onward(2, p2)
     v1 = relay(1, vb, v1, 1)
     m = m + mix(1, v1, p1)
     v2 = relay(1, vb, v2, 2)
@@ -396,8 +431,8 @@
             f32(D // 128, T, 128), f32(256, D), bf(256, D), bf(256, D), bf(256, D), bf(256, D), bf(256, D),
             f32(256, D), bf(2, NS, 32, D), bf(2, NS, 32, D), f32(64, 128),
             pltpu.SemaphoreType.DMA((10,)),
-        ] + pairs_of(3, HG, NY - 1) + pairs_of(2, HG, 3) + pairs_of(HG, NZ - 1) + pairs_of(HG)
-        + pairs_of(HG, NZ - 1) + pairs_of(HG, NY - 1) + pairs_of(2, NS - 1) + pairs_of(2, NS - 1),
+        ] + pairs_of(3, HG, NY - 1) + pairs_of(2, HG, 3) + pairs_of(2, NY) + pairs_of(HG, NZ - 1)
+        + pairs_of(HG) + pairs_of(HG, 4) + pairs_of(HG, NY - 1) + pairs_of(2, NS - 1) + pairs_of(2, NS - 1),
         compiler_params=pltpu.CompilerParams(
             collective_id=0, has_side_effects=True, vmem_limit_bytes=VMEM_LIMIT
         ),

time: 106 us -> 102 us (0.962); the launches traced: 104 us -> 102 us
  Pallas kernels: 102 us -> 100 us
    pallas_call x1, Pallas kernels: 102 us -> 100 us  [local(): pl.pallas_call(layer_kernel, out_shape=jax.ShapeDtypeStruct((T, D), BF),...]
where the time goes in v6:
time: 102 us
  Pallas kernels  100 us (98%)
  local copies, waits for them, and re-layouts  2.06 us (2%)
    pallas_call x1, Pallas kernels, local(): pl.pallas_call(layer_kernel, out_shape=jax.ShapeDtypeStruct((T, D), BF),...  100 us
    unnamed x1, local copies, waits for them, and re-layouts  2.06 us

profile of v6, /device:TPU:8, one launch (start us, length us, event | category | flops | bytes accessed | tf_op | source)
XLA Modules:
  0.0 102.1 jit_solution(12045713760165165883)
XLA Ops:
  0.0 100.1 %layer.1 = bf16[512,768]{1,0:T(8,128)(2,1)} custom-call(s32[64]{0:T(128)} %mask.1, bf16[512,768]{1,0:T(8,128)(2,1)} %bitcast.3, bf16[768]{0:T(1024)(128)(2,1)} %gr.1, bf16[768]{0:T(1024)(128)(2,1)} %gc.1, bf16[768]{0:T(1024)(128)(2,1)} %gf.1, bf16[768,768]{1,0:T(8,128)(2,1)} %rq_h.1, bf16[768,768]{1,0:T(8,128)(2,1)} %rk_h.1, bf16[768,768]{1,0:T(8,128)(2,1)} %rv_h.1, ...), custom_call_target="tpu_custom_call" | custom-call | tf_op jit(solution)/shard_map/layer/pallas_call | solution.py:418
  100.1 2.1 %copy.17 = bf16[8,64,768]{2,1,0:T(8,128)(2,1)} copy(bf16[8,64,768]{2,1,0:T(8,128)(2,1)} %bitcast.2) | data formatting | bytes 1572864

commit v7 on v6

--- a/solution.py
+++ b/solution.py
@@ -86,8 +86,8 @@
 
 
 def layer_kernel(
-    mask, x, gr, gc, gf, rq_h, rk_h, rv_h, ro_h, cq_h, ck_h, cv_h, co_h, up_h, dn_h, out,
-    wrk, wrq, wrv, wro, wcq, wck, wcv, wco, up, dn,
+    mask_h, x, gr, gc, gf, rq_h, rk_h, rv_h, ro_h, cq_h, ck_h, cv_h, co_h, up_h, dn_h, out,
+    mask, wrk, wrq, wrv, wro, wcq, wck, wcv, wco, up, dn,
     xn, acc, pk, qb, kb, vb, part, pb, rs, th, xs, xr, pw, mxs, mxr, cs, ci,
     xf, xo, cin, qc, kc, vc, hb, facc, co, cr, bias,
     lsem, ys, yr, fs, fr, ps, pr, zs, zr, hs, hr, as_, ar, ms, mr, cs_s, cs_r, os_, or_,
@@ -112,6 +112,8 @@
         (co_h, wco), (up_h, up), (dn_h, dn),
     )
     loads = [Load(h, v, lsem.at[i]) for i, (h, v) in enumerate(pairs)]
+    mask_load = Load(mask_h, mask, lsem.at[10])
+    loads.append(mask_load)
     barrier = pltpu.get_barrier_semaphore()
     peers = ydev[1:] + [far, core] + sdev[1:]
     for peer in peers:
@@ -244,6 +246,7 @@
     pl.semaphore_wait(barrier, len(peers))
     ky[0] = over_y(0, kb, own, 0)
     k0 = [piece(y, 0)]
+    mask_load.wait()
     project(1, wrq, loads[1], masked=True)
     ky[1] = over_y(0, kb, own, 1)
     qy[0] = over_y(1, qb, y, 0)
@@ -351,12 +354,7 @@
             load.wait()
             into[...] = dot(cin[...], weight[...]).astype(BF)
 
-        @pl.loop(0, 2)
-        def _(step):
-            attend([
-                (chunk(step * 2 + c, 64), slice(g * 256, (g + 1) * 256)) for c in range(2) for g in range(3)
-            ])
-
+        attend([(slice(c * 64, (c + 1) * 64), slice(g * 256, (g + 1) * 256)) for c in range(4) for g in range(3)])
         loads[7].wait()
         after = (xo[...] + dot(cin[...], wco[...])).astype(BF).astype(F32)
         facc[...] = after
@@ -418,9 +416,9 @@
     out = pl.pallas_call(
         layer_kernel,
         out_shape=jax.ShapeDtypeStruct((T, D), BF),
-        in_specs=[pl.BlockSpec(memory_space=pltpu.SMEM)] + [vmem()] * 4 + [hbm()] * 10,
+        in_specs=[hbm()] + [vmem()] * 4 + [hbm()] * 10,
         out_specs=vmem(),
-        scratch_shapes=[bf(D, D)] * 8 + [
+        scratch_shapes=[pltpu.SMEM((NS * RL,), jnp.int32)] + [bf(D, D)] * 8 + [
             bf(D, FF), bf(FF, D),
             bf(T, D), f32(T, D), bf(3, H, CL, 512),
             bf(HG, 256, 512), bf(HG, 1024, 512), bf(HG, 1024, 512),
@@ -430,7 +428,7 @@
             bf(2, NS, 32, D), bf(2, NS, 32, D),
             f32(D // 128, T, 128), f32(256, D), bf(256, D), bf(256, D), bf(256, D), bf(256, D), bf(256, D),
             f32(256, D), bf(2, NS, 32, D), bf(2, NS, 32, D), f32(64, 128),
-            pltpu.SemaphoreType.DMA((10,)),
+            pltpu.SemaphoreType.DMA((11,)),
         ] + pairs_of(3, HG, NY - 1) + pairs_of(2, HG, 3) + pairs_of(2, NY) + pairs_of(HG, NZ - 1)
         + pairs_of(HG) + pairs_of(HG, 4) + pairs_of(HG, NY - 1) + pairs_of(2, NS - 1) + pairs_of(2, NS - 1),
         compiler_params=pltpu.CompilerParams(

time: 102 us -> 102 us (level)
  no operation moved by 1% of the time
where the time goes in v7:
time: 102 us; the launch traced here: 101 us
  Pallas kernels  99.3 us (97%)
  local copies, waits for them, and re-layouts  2.06 us (2%)
    pallas_call x1, Pallas kernels, local(): pl.pallas_call(layer_kernel, out_shape=jax.ShapeDtypeStruct((T, D), BF),...  99.3 us
    unnamed x1, local copies, waits for them, and re-layouts  2.06 us

profile of v7, /device:TPU:8, one launch (start us, length us, event | category | flops | bytes accessed | tf_op | source)
XLA Modules:
  0.0 101.4 jit_solution(16020162707855243822)
XLA Ops:
  0.0 99.3 %layer.1 = bf16[512,768]{1,0:T(8,128)(2,1)} custom-call(s32[64]{0:T(128)} %mask_h.1, bf16[512,768]{1,0:T(8,128)(2,1)} %bitcast.3, bf16[768]{0:T(1024)(128)(2,1)} %gr.1, bf16[768]{0:T(1024)(128)(2,1)} %gc.1, bf16[768]{0:T(1024)(128)(2,1)} %gf.1, bf16[768,768]{1,0:T(8,128)(2,1)} %rq_h.1, bf16[768,768]{1,0:T(8,128)(2,1)} %rk_h.1, bf16[768,768]{1,0:T(8,128)(2,1)} %rv_h.1, ...), custom_call_target="tpu_custom_call" | custom-call | tf_op jit(solution)/shard_map/layer/pallas_call | solution.py:416
  99.3 2.1 %copy.17 = bf16[8,64,768]{2,1,0:T(8,128)(2,1)} copy(bf16[8,64,768]{2,1,0:T(8,128)(2,1)} %bitcast.2) | data formatting | bytes 1572864
